TPU v7x, 32 devices: a whole 2x2x4 slice. The times are simulated.
32 devices in a mesh: dp: 8 (over z, y), row: 2 (over core), col: 2 (over x).
Axes of the slice: x: 2, y: 2, z: 4, core: 2. Of those that a mesh axis runs over, the one named last changes fastest.
Arguments:
- tokens: bfloat16 [8192, 1024], P('dp', ('row', 'col')), may hold values from -6 to 6
- lengths: int32 [8, 3], P('dp'), may hold values from 1 to 512, 1024 in all within a row
- ln1_gain: float32 [1024], P(('row', 'col')), may hold values from 0.25 to 1.75
- ln1_shift: float32 [1024], P(('row', 'col')), may hold values from -3 to 3
- w_qkv: bfloat16 [1024, 3072], P('row', 'col'), may hold values from -0.1875 to 0.1875
- b_qv: float32 [2048], P('col'), may hold values from -3 to 3
- w_out: bfloat16 [1024, 1024], P('col', 'row'), may hold values from -0.75 to 0.75
- b_out: float32 [1024], P(('row', 'col')), may hold values from -3 to 3
- ln2_gain: float32 [1024], P(('row', 'col')), may hold values from 0.25 to 1.75
- ln2_shift: float32 [1024], P(('row', 'col')), may hold values from -3 to 3
- w_up: bfloat16 [1024, 4096], P('row', 'col'), may hold values from -0.1875 to 0.1875
- b_up: float32 [4096], P('col'), may hold values from -3 to 3
- w_down: bfloat16 [4096, 1024], P('col', 'row'), may hold values from -0.09375 to 0.09375
- b_down: float32 [1024], P(('row', 'col')), may hold values from -3 to 3
- cotangent: bfloat16 [8192, 1024], P('dp', ('row', 'col')), may hold values from -6 to 6
Outputs:
- block_out: bfloat16 [8192, 1024], P('dp', ('row', 'col'))
- grad_input: float32 [8192, 1024], P('dp', ('row', 'col'))
- grad_ln1_gain: float32 [1024], P(('row', 'col'))
- grad_ln1_shift: float32 [1024], P(('row', 'col'))
- grad_w_qkv: float32 [1024, 3072], P('row', 'col')
- grad_b_qv: float32 [2048], P('col')
- grad_w_out: float32 [1024, 1024], P('col', 'row')
- grad_b_out: float32 [1024], P(('row', 'col'))
- grad_ln2_gain: float32 [1024], P(('row', 'col'))
- grad_ln2_shift: float32 [1024], P(('row', 'col'))
- grad_w_up: float32 [1024, 4096], P('row', 'col')
- grad_b_up: float32 [4096], P('col')
- grad_w_down: float32 [4096, 1024], P('col', 'row')
- grad_b_down: float32 [1024], P(('row', 'col'))
Inputs may be any that keep to these rules, and one draw needn't show every extreme that they name: Row g lists in order the lengths of the sequences packed into the 1024 tokens of data group g; each row sums to 1024 and its longest is exactly 512.
All inputs are finite; a program needn't handle non-finite values.
Results may differ from a plain program's by a relative error of at most 0.0093.
Values may be sent and summed in bfloat16 or wider, within the bound.
A program may use at most 128 MiB of HBM per device.

v0:
```python
import jax
import jax.numpy as jnp
from jax import lax
from jax.sharding import PartitionSpec as P

HEADS = 16
HEAD_DIM = 64
QB = 512
KW = 1024


EPSILON = 1e-05


def norm_forward(values, gain, shift):
    width = values.shape[1] * lax.axis_size(("row", "col"))
    sums = lax.psum((jnp.sum(values, axis=1), jnp.sum(values * values, axis=1)), ("row", "col"))
    center = sums[0] / width
    spread = sums[1] / width - center * center
    scaled = lax.rsqrt(spread + EPSILON)
    unit = (values - center[:, None]) * scaled[:, None]
    return (unit * gain + shift, unit, scaled)


def norm_backward(grad_normed, unit, scaled, gain):
    width = unit.shape[1] * lax.axis_size(("row", "col"))
    grad_gain = jnp.sum(grad_normed * unit, axis=0)
    grad_shift = jnp.sum(grad_normed, axis=0)
    scaled_grad = grad_normed * gain
    sums = lax.psum(
        (jnp.sum(scaled_grad, axis=1), jnp.sum(scaled_grad * unit, axis=1)), ("row", "col")
    )
    grad_values = scaled[:, None] * (
        scaled_grad - sums[0][:, None] / width - unit * (sums[1][:, None] / width)
    )
    return (grad_values, grad_gain, grad_shift)


def feature_gather(values):
    return lax.all_gather(values, "col", axis=1, tiled=True)


def unit_reduce(values):
    return lax.psum_scatter(values, "row", scatter_dimension=1, tiled=True)


def unit_gather(values):
    return lax.all_gather(values, "row", axis=1, tiled=True)


def width_reduce(values):
    return lax.psum_scatter(values, "col", scatter_dimension=1, tiled=True)


def grad_feature_gather(values):
    return lax.all_gather(values, "col", axis=1, tiled=True)


def grad_unit_reduce(values):
    return lax.psum_scatter(values, "row", scatter_dimension=1, tiled=True)


def grad_unit_gather(values):
    return lax.all_gather(values, "row", axis=1, tiled=True)


def grad_width_reduce(values):
    return lax.psum_scatter(values, "col", scatter_dimension=1, tiled=True)


def project_own(normed, weight_block):
    gathered = feature_gather(normed)
    product = unit_reduce(jnp.dot(gathered, weight_block, preferred_element_type=jnp.float32))
    return (product, gathered)


def block_scores(queries, key_rows, segment, slopes, offset):
    row_count = queries.shape[0]
    scale = queries.shape[2] ** (-0.5)
    key_first = jnp.clip(offset + QB - KW, 0, row_count - KW)
    query_block = lax.dynamic_slice_in_dim(queries, offset, QB, 0)
    query_place = offset + jnp.arange(QB, dtype=jnp.int32)
    key_place = key_first + jnp.arange(KW, dtype=jnp.int32)
    query_seg = lax.dynamic_slice_in_dim(segment, offset, QB, 0)
    allowed = (query_seg[:, None] == segment[None, :]) & (
        key_place[None, :] <= query_place[:, None]
    )
    distance = (query_place[:, None] - key_place[None, :]).astype(jnp.float32)
    scores = (
        jnp.einsum("qhd,khd->hqk", query_block, key_rows, preferred_element_type=jnp.float32)
        * scale
    )
    scores = scores - slopes[:, None, None] * distance[None]
    return (jnp.where(allowed[None], scores, -1000000000.0), key_first, query_block, key_rows)


def attend_forward(queries, key_rows, value_rows, segment, slopes):
    row_count, heads, width = queries.shape
    starts = jnp.arange(row_count // QB, dtype=jnp.int32) * QB

    def one_block(offset):
        scores, key_first, query_block, key_block = block_scores(
            queries, key_rows, segment, slopes, offset
        )
        ceiling = jnp.max(scores, axis=-1, keepdims=True)
        weights = jnp.exp(scores - ceiling)
        totals = jnp.sum(weights, axis=-1, keepdims=True)
        weights = weights / totals
        context = jnp.einsum(
            "hqk,khd->qhd",
            weights.astype(jnp.bfloat16),
            value_rows,
            preferred_element_type=jnp.float32,
        )
        return (context, (ceiling + jnp.log(totals))[:, :, 0])

    context, logsum = lax.map(one_block, starts)
    return (
        context.reshape(row_count, heads, width),
        jnp.transpose(logsum, (1, 0, 2)).reshape(heads, row_count),
    )


def attend_backward(queries, key_rows, value_rows, grad_context, logsum, segment, slopes):
    row_count, heads, width = queries.shape
    scale = width ** (-0.5)
    starts = jnp.arange(row_count // QB, dtype=jnp.int32) * QB

    def one_block(carry, offset):
        grad_keys, grad_values = carry
        scores, key_first, query_block, key_block = block_scores(
            queries, key_rows, segment, slopes, offset
        )
        weights = jnp.exp(scores - lax.dynamic_slice_in_dim(logsum, offset, QB, 1)[:, :, None])
        grad_block = lax.dynamic_slice_in_dim(grad_context, offset, QB, 0)
        grad_weights = jnp.einsum(
            "qhd,khd->hqk", grad_block, value_rows, preferred_element_type=jnp.float32
        )
        inner = jnp.sum(weights * grad_weights, axis=-1, keepdims=True)
        grad_scores = (weights * (grad_weights - inner)).astype(jnp.bfloat16)
        grad_query = (
            jnp.einsum("hqk,khd->qhd", grad_scores, key_block, preferred_element_type=jnp.float32)
            * scale
        )
        grad_key = (
            jnp.einsum("hqk,qhd->khd", grad_scores, query_block, preferred_element_type=jnp.float32)
            * scale
        )
        grad_value = jnp.einsum(
            "hqk,qhd->khd",
            weights.astype(jnp.bfloat16),
            grad_block,
            preferred_element_type=jnp.float32,
        )
        grad_keys = grad_keys + grad_key
        grad_values = grad_values + grad_value
        return ((grad_keys, grad_values), grad_query)

    zeros = jnp.zeros((row_count, heads, width), jnp.float32)
    (grad_keys, grad_values), grad_queries = lax.scan(one_block, (zeros, zeros), starts)
    return (grad_queries.reshape(row_count, heads, width), grad_keys, grad_values)


def shards(
    tokens,
    lengths,
    ln1_gain,
    ln1_shift,
    w_qkv,
    b_qv,
    w_out,
    b_out,
    ln2_gain,
    ln2_shift,
    w_up,
    b_up,
    w_down,
    b_down,
    cotangent,
):
    row_count = tokens.shape[0]
    row_index = lax.axis_index("row")
    col_index = lax.axis_index("col")
    row_devices = lax.axis_size("row")
    col_heads = w_qkv.shape[1] // (3 * HEAD_DIM)
    local_heads = col_heads // row_devices
    ends = jnp.cumsum(lengths[0])
    places = jnp.arange(row_count, dtype=jnp.int32)
    segment = jnp.sum((places[:, None] >= ends[None, :]).astype(jnp.int32), axis=1)
    head_ids = (
        col_index * col_heads + row_index * local_heads + jnp.arange(local_heads, dtype=jnp.int32)
    ).astype(jnp.float32)
    slopes = jnp.exp2(-8.0 * (head_ids + 1.0) / HEADS)
    inputs = tokens.astype(jnp.float32)
    normed1, unit1, scaled1 = norm_forward(inputs, ln1_gain, ln1_shift)
    mixed, gathered1 = project_own(normed1.astype(jnp.bfloat16), w_qkv)
    pair_bias = lax.dynamic_slice_in_dim(
        b_qv.reshape(col_heads, 2, HEAD_DIM), row_index * local_heads, local_heads, 0
    )
    joined_bias = jnp.stack(
        [pair_bias[:, 0], jnp.zeros_like(pair_bias[:, 0]), pair_bias[:, 1]], axis=1
    ).reshape(-1)
    mixed = (mixed + joined_bias).astype(jnp.bfloat16).reshape(row_count, local_heads, 3, HEAD_DIM)
    queries = mixed[:, :, 0]
    key_rows = mixed[:, :, 1]
    value_rows = mixed[:, :, 2]
    context, logsum = attend_forward(queries, key_rows, value_rows, segment, slopes)
    context_rows = unit_gather(
        context.reshape(row_count, local_heads * HEAD_DIM).astype(jnp.bfloat16)
    )
    after = (
        inputs
        + width_reduce(jnp.dot(context_rows, w_out, preferred_element_type=jnp.float32))
        + b_out
    )
    normed2, unit2, scaled2 = norm_forward(after, ln2_gain, ln2_shift)
    pre_width = w_up.shape[1] // row_devices
    preact, gathered2 = project_own(normed2.astype(jnp.bfloat16), w_up)
    preact = preact + lax.dynamic_slice_in_dim(b_up, row_index * pre_width, pre_width, 0)
    active_rows = unit_gather(jax.nn.gelu(preact, approximate=True).astype(jnp.bfloat16))
    result = (
        after
        + width_reduce(jnp.dot(active_rows, w_down, preferred_element_type=jnp.float32))
        + b_down
    )
    block_out = result.astype(jnp.bfloat16)
    grad_out = cotangent.astype(jnp.float32)
    grad_rows = grad_feature_gather(cotangent)
    grad_w_down = jnp.einsum(
        "ti,to->io", active_rows, grad_rows, preferred_element_type=jnp.float32
    )
    grad_b_down = jnp.sum(grad_out, axis=0)
    grad_active = grad_unit_reduce(
        jnp.einsum("to,io->ti", grad_rows, w_down, preferred_element_type=jnp.float32)
    )
    unused, gelu_pull = jax.vjp(lambda values: jax.nn.gelu(values, approximate=True), preact)
    grad_pre = gelu_pull(grad_active)[0].astype(jnp.bfloat16)
    grad_pre_rows = grad_unit_gather(grad_pre)
    grad_w_up = jnp.einsum(
        "ti,to->io", gathered2, grad_pre_rows, preferred_element_type=jnp.float32
    )
    grad_b_up = jnp.sum(grad_pre_rows, axis=0, dtype=jnp.float32)
    grad_normed2 = grad_width_reduce(
        jnp.einsum("to,io->ti", grad_pre_rows, w_up, preferred_element_type=jnp.float32)
    )
    grad_after_norm, grad_ln2_gain, grad_ln2_shift = norm_backward(
        grad_normed2, unit2, scaled2, ln2_gain
    )
    grad_after = grad_out + grad_after_norm
    grad_after_rows = grad_feature_gather(grad_after.astype(jnp.bfloat16))
    grad_w_out = jnp.einsum(
        "ti,to->io", context_rows, grad_after_rows, preferred_element_type=jnp.float32
    )
    grad_b_out = jnp.sum(grad_after, axis=0)
    grad_context = grad_unit_reduce(
        jnp.einsum("to,io->ti", grad_after_rows, w_out, preferred_element_type=jnp.float32)
    )
    grad_context = grad_context.astype(jnp.bfloat16).reshape(row_count, local_heads, HEAD_DIM)
    grad_queries, grad_keys, grad_values = attend_backward(
        queries, key_rows, value_rows, grad_context, logsum, segment, slopes
    )
    grad_mixed = jnp.stack([grad_queries, grad_keys, grad_values], axis=2).reshape(
        row_count, local_heads * 3 * HEAD_DIM
    )
    grad_mixed_rows = grad_unit_gather(grad_mixed.astype(jnp.bfloat16))
    grad_w_qkv = jnp.einsum(
        "ti,to->io", gathered1, grad_mixed_rows, preferred_element_type=jnp.float32
    )
    column_sums = jnp.sum(grad_mixed_rows, axis=0, dtype=jnp.float32).reshape(
        col_heads, 3, HEAD_DIM
    )
    grad_b_qv = jnp.stack([column_sums[:, 0], column_sums[:, 2]], axis=1).reshape(-1)
    grad_normed1 = grad_width_reduce(
        jnp.einsum("to,io->ti", grad_mixed_rows, w_qkv, preferred_element_type=jnp.float32)
    )
    grad_input_norm, grad_ln1_gain, grad_ln1_shift = norm_backward(
        grad_normed1, unit1, scaled1, ln1_gain
    )
    grad_input = grad_after + grad_input_norm
    (
        grad_ln1_gain,
        grad_ln1_shift,
        grad_w_qkv,
        grad_b_qv,
        grad_w_out,
        grad_b_out,
        grad_ln2_gain,
        grad_ln2_shift,
        grad_w_up,
        grad_b_up,
        grad_w_down,
        grad_b_down,
    ) = lax.psum(
        (
            grad_ln1_gain,
            grad_ln1_shift,
            grad_w_qkv,
            grad_b_qv,
            grad_w_out,
            grad_b_out,
            grad_ln2_gain,
            grad_ln2_shift,
            grad_w_up,
            grad_b_up,
            grad_w_down,
            grad_b_down,
        ),
        "dp",
    )
    return (
        block_out,
        grad_input,
        grad_ln1_gain,
        grad_ln1_shift,
        grad_w_qkv,
        grad_b_qv,
        grad_w_out,
        grad_b_out,
        grad_ln2_gain,
        grad_ln2_shift,
        grad_w_up,
        grad_b_up,
        grad_w_down,
        grad_b_down,
    )


def solution(mesh):
    in_specs = (
        P("dp", ("row", "col")),
        P("dp", None),
        P(("row", "col")),
        P(("row", "col")),
        P("row", "col"),
        P("col"),
        P("col", "row"),
        P(("row", "col")),
        P(("row", "col")),
        P(("row", "col")),
        P("row", "col"),
        P("col"),
        P("col", "row"),
        P(("row", "col")),
        P("dp", ("row", "col")),
    )
    out_specs = (
        P("dp", ("row", "col")),
        P("dp", ("row", "col")),
        P(("row", "col")),
        P(("row", "col")),
        P("row", "col"),
        P("col"),
        P("col", "row"),
        P(("row", "col")),
        P(("row", "col")),
        P(("row", "col")),
        P("row", "col"),
        P("col"),
        P("col", "row"),
        P(("row", "col")),
    )
    return jax.shard_map(shards, mesh=mesh, in_specs=in_specs, out_specs=out_specs, check_vma=False)
```

profile of v0, /device:TPU:0, one launch (start us, length us, event | category | flops | bytes accessed | tf_op | source)
XLA Modules:
  0.0 907.5 jit_solution(8465025821100434816)
XLA Ops:
  8.8 9.0 all-reduce.5
  20.1 22.3 %all-gather.9.cloned.1.call-done = bf16[1024,512]{1,0:T(8,128)(2,1)} async-done(((bf16[1024,256]{1,0:T(8,128)(2,1)}), bf16[1024,512]{1,0:T(8,128)(2,1)}) %all-gather.9.cloned.1.call-update) | async-done | bytes 1048592 | tf_op jit(solution)/shard_map/all_gather | solution.py:40
  49.8 13.5 %reduce-scatter.9.cloned.1.call-done = f32[1024,768]{1,0:T(8,128)} async-done(((f32[1024,1536]{1,0:T(8,128)}), f32[1024,768]{1,0:T(8,128)}) %reduce-scatter.9.cloned.1.call-update) | async-done | bytes 3145744 | tf_op jit(solution)/shard_map/reduce_scatter | solution.py:44
  72.3 32.3 %while.36 = (s32[]{:T(128)}, bf16[2,512,4,64]{1,3,2,0:T(8,128)(2,1)}, f32[2,4,512]{2,1,0:T(4,128)S(1)}, s32[2]{0:T(128)S(1)}, s32[1024]{0:T(1024)S(1)}, /*index=...) while((s32[]{:T(128)}, ...), condition=%wide.region_10.11_spmd.clone, body=%wide.region_7.10_spmd.clone.sunk | while | flops 577240576 | bytes 41776456 | solution.py:117
  107.2 10.3 %all-gather.11.cloned.1.call-done = bf16[1024,512]{0,1:T(8,128)(2,1)} async-done(((bf16[1024,256]{0,1:T(8,128)(2,1)}), bf16[1024,512]{0,1:T(8,128)(2,1)}) %all-gather.11.cloned.1.call-update) | async-done | bytes 1048592 | tf_op jit(solution)/shard_map/all_gather | solution.py:48
  121.5 32.5 %reduce-scatter.11.cloned.1.call-done = f32[1024,256]{1,0:T(8,128)} async-done(((f32[1024,512]{1,0:T(8,128)}), f32[1024,256]{1,0:T(8,128)}) %reduce-scatter.11.cloned.1.call-update) | async-done | bytes 1048592 | tf_op jit(solution)/shard_map/reduce_scatter | solution.py:52
  165.6 11.1 %all-gather.17.cloned.1.call-done = bf16[1024,512]{1,0:T(8,128)(2,1)} async-done(((bf16[1024,256]{1,0:T(8,128)(2,1)}), bf16[1024,512]{1,0:T(8,128)(2,1)}) %all-gather.17.cloned.1.call-update) | async-done | bytes 1048592 | tf_op jit(solution)/shard_map/all_gather | solution.py:56
  176.7 7.5 fusion.64
  184.3 15.7 %all-gather.13.cloned.1.call-done = bf16[1024,512]{1,0:T(8,128)(2,1)} async-done(((bf16[1024,256]{1,0:T(8,128)(2,1)}), bf16[1024,512]{1,0:T(8,128)(2,1)}) %all-gather.13.cloned.1.call-update) | async-done | bytes 1048592 | tf_op jit(solution)/shard_map/all_gather | solution.py:40
  200.0 6.8 fusion.62
  207.5 11.7 %reduce-scatter.17.cloned.1.call-done = f32[1024,1024]{1,0:T(8,128)} async-done(((f32[1024,2048]{1,0:T(8,128)}), f32[1024,1024]{1,0:T(8,128)}) %reduce-scatter.17.cloned.1.call-update) | async-done | bytes 4194320 | tf_op jit(solution)/shard_map/reduce_scatter | solution.py:60
  219.2 20.5 %reduce-scatter.13.cloned.1.call-done = f32[1024,1024]{1,0:T(8,128)} async-done(((f32[1024,2048]{1,0:T(8,128)}), f32[1024,1024]{1,0:T(8,128)}) %reduce-scatter.13.cloned.1.call-update) | async-done | bytes 4194320 | tf_op jit(solution)/shard_map/reduce_scatter | solution.py:44
  247.0 14.5 %all-gather.19.cloned.1.call-done = bf16[1024,2048]{1,0:T(8,128)(2,1)} async-done(((bf16[1024,1024]{1,0:T(8,128)(2,1)}), bf16[1024,2048]{1,0:T(8,128)(2,1)}) %all-gather.19.cloned.1.call-update) | async-done | bytes 4194320 | tf_op jit(solution)/shard_map/all_gather | solution.py:64
  267.4 10.9 %all-gather.15.cloned.1.call-done = bf16[1024,2048]{1,0:T(8,128)(2,1)} async-done(((bf16[1024,1024]{1,0:T(8,128)(2,1)}), bf16[1024,2048]{1,0:T(8,128)(2,1)}) %all-gather.15.cloned.1.call-update) | async-done | bytes 4194320 | tf_op jit(solution)/shard_map/all_gather | solution.py:48
  284.9 29.3 %reduce-scatter.19.cloned.1.call-done = f32[1024,256]{1,0:T(8,128)} async-done(((f32[1024,512]{1,0:T(8,128)}), f32[1024,256]{1,0:T(8,128)}) %reduce-scatter.19.cloned.1.call-update) | async-done | bytes 1048592 | tf_op jit(solution)/shard_map/reduce_scatter | solution.py:68
  322.5 26.3 %reduce-scatter.15.cloned.1.call-done = f32[1024,256]{1,0:T(8,128)} async-done(((f32[1024,512]{1,0:T(8,128)}), f32[1024,256]{1,0:T(8,128)}) %reduce-scatter.15.cloned.1.call-update) | async-done | bytes 1048592 | tf_op jit(solution)/shard_map/reduce_scatter | solution.py:52
  352.6 21.4 %all-gather.21.cloned.1.call-done = bf16[1024,512]{1,0:T(8,128)(2,1)} async-done(((bf16[1024,256]{1,0:T(8,128)(2,1)}), bf16[1024,512]{1,0:T(8,128)(2,1)}) %all-gather.21.cloned.1.call-update) | async-done | bytes 1048592 | tf_op jit(solution)/shard_map/all_gather | solution.py:56
  377.7 9.5 %reduce-scatter.21.cloned.1.call-done = f32[1024,256]{1,0:T(8,128)} async-done(((f32[1024,512]{1,0:T(8,128)}), f32[1024,256]{1,0:T(8,128)}) %reduce-scatter.21.cloned.1.call-update) | async-done | bytes 1048592 | tf_op jit(solution)/shard_map/reduce_scatter | solution.py:60
  392.1 33.9 %while.37 = (s32[]{:T(128)}, f32[1024,4,64]{0,2,1:T(8,128)S(1)}, f32[1024,4,64]{0,2,1:T(8,128)}, bf16[2,512,4,64]{1,3,2,0:T(8,128)(2,1)}, s32[2]{0:T(128)S(1)}, ...) while((s32[]{:T(128)}, f32[1024,4,64]{0,2,1:T(8,128)S(1)}, ...), condition=%wide.region_27.28_spmd.clone, body=%wide.region_25.27_spmd.clone.sunk | while | flops 1369308672 | bytes 88150944 | solution.py:160
  431.9 13.2 %all-gather.23.cloned.1.call-done = bf16[1024,1536]{0,1:T(8,128)(2,1)} async-done(((bf16[1024,768]{0,1:T(8,128)(2,1)}), bf16[1024,1536]{0,1:T(8,128)(2,1)}) %all-gather.23.cloned.1.call-update) | async-done | bytes 3145744 | tf_op jit(solution)/shard_map/all_gather | solution.py:64
  472.2 11.0 %reduce-scatter.23.cloned.1.call-done = f32[1024,256]{1,0:T(8,128)} async-done(((f32[1024,512]{1,0:T(8,128)}), f32[1024,256]{1,0:T(8,128)}) %reduce-scatter.23.cloned.1.call-update) | async-done | bytes 1048592 | tf_op jit(solution)/shard_map/reduce_scatter | solution.py:68
  485.2 39.1 %all-reduce = (f32[256]{0:T(256)}, f32[256]{0:T(256)}, f32[1024]{0:T(1024)}, f32[256]{0:T(256)}, f32[256]{0:T(256)}, /*index=5*/f32[256]{0:T(256)}, f32[2048]{0:T(1024)}, f32[256]{0:T(256)}) all-reduce(f32[256]{0:T(256)S(1)} %get-tuple-element.514, f32[256]{0:T(256)S(1)} %get-tuple-element.519, ...), channel_id=1, replica_groups=mesh['dp'=8,'row'=2,'col'=2] {'dp'}, use_global_device_ids=true, to_apply=%region_34.35 | all-reduce | flops 4608 | bytes 36864 | tf_op jit(solution)/shard_map/psum | solution.py:293
  524.3 6.9 all-reduce.2
  533.9 356.0 %all-reduce.8.cloned.1.call-done = (f32[512,1536]{1,0:T(8,128)}, f32[512,512]{1,0:T(8,128)}, f32[512,2048]{1,0:T(8,128)}, f32[2048,512]{1,0:T(8,128)}) async-done(((f32[512,1536]{1,0:T(8,128)}, f32[512,512]{1,0:T(8,128)}, f32[512,2048]{1,0:T(8,128)}, f32[2048,512]{1,0:T(8,128)}), (f32[512,1536]{1,0:T(8,128)}, f32[512,512]{1,0:T(8,128)}, f32[512,2048]{1,0:T(8,128)}, ...) | async-done | bytes 12582928 | tf_op jit(solution)/shard_map/psum | solution.py:293
  (232 shorter events, 183.0 us)
Async XLA Ops:
  7.2 192.8 %copy-start = (bf16[512,2048]{1,0:T(8,128)(2,1)S(1)}, bf16[512,2048]{1,0:T(8,128)(2,1)}, u32[]{:S(2)}) copy-start(bf16[512,2048]{1,0:T(8,128)(2,1)} %param.29) | copy-start | bytes 6291460
  7.2 35.2 %all-gather.9.cloned.1.call-start = ((), (), s32[]{:S(2)}) async-start(), calls=%async_computation.8 | async-start | bytes 1572864 | tf_op jit(solution)/shard_map/all_gather | solution.py:40
  20.1 43.2 %reduce-scatter.9.cloned.1.call-start = ((), (), s32[]{:S(2)}) async-start(), calls=%async_computation.9 | async-start | bytes 9437184 | tf_op jit(solution)/shard_map/reduce_scatter | solution.py:44
  48.6 68.8 %all-gather.11.cloned.1.call-start = ((), (), s32[]{:S(2)}) async-start(), calls=%async_computation.10 | async-start | bytes 1572864 | tf_op jit(solution)/shard_map/all_gather | solution.py:48
  106.2 47.9 %copy-start.29 = (f32[256]{0:T(256)S(1)}, f32[256]{0:T(256)}, u32[]{:S(2)}) copy-start(f32[256]{0:T(256)} %param.26) | copy-start | bytes 3076
  107.1 56.0 %copy-start.25 = (f32[256]{0:T(256)S(1)}, f32[256]{0:T(256)}, u32[]{:S(2)}) copy-start(f32[256]{0:T(256)} %param.27) | copy-start | bytes 3076
  107.1 56.0 %copy-start.30 = (f32[256]{0:T(256)S(1)}, f32[256]{0:T(256)}, u32[]{:S(2)}) copy-start(f32[256]{0:T(256)} %param.28) | copy-start | bytes 3076
  107.1 46.9 %reduce-scatter.11.cloned.1.call-start = ((), (), s32[]{:S(2)}) async-start(), calls=%async_computation.11 | async-start | bytes 3145728 | tf_op jit(solution)/shard_map/reduce_scatter | solution.py:52
  120.9 55.8 %all-gather.17.cloned.1.call-start = ((), (), s32[]{:S(2)}) async-start(), calls=%async_computation.16 | async-start | bytes 1572864 | tf_op jit(solution)/shard_map/all_gather | solution.py:56
  121.5 78.5 %all-gather.13.cloned.1.call-start = ((), (), s32[]{:S(2)}) async-start(), calls=%async_computation.12 | async-start | bytes 1572864 | tf_op jit(solution)/shard_map/all_gather | solution.py:40
  165.5 53.6 %reduce-scatter.17.cloned.1.call-start = ((), (), s32[]{:S(2)}) async-start(), calls=%async_computation.17 | async-start | bytes 12582912 | tf_op jit(solution)/shard_map/reduce_scatter | solution.py:60
  184.3 55.4 %reduce-scatter.13.cloned.1.call-start = ((), (), s32[]{:S(2)}) async-start(), calls=%async_computation.13 | async-start | bytes 12582912 | tf_op jit(solution)/shard_map/reduce_scatter | solution.py:44
  206.8 54.6 %all-gather.19.cloned.1.call-start = ((), (), s32[]{:S(2)}) async-start(), calls=%async_computation.18 | async-start | bytes 6291456 | tf_op jit(solution)/shard_map/all_gather | solution.py:64
  246.4 31.9 %all-gather.15.cloned.1.call-start = ((), (), s32[]{:S(2)}) async-start(), calls=%async_computation.14 | async-start | bytes 6291456 | tf_op jit(solution)/shard_map/all_gather | solution.py:48
  246.9 67.2 %reduce-scatter.19.cloned.1.call-start = ((), (), s32[]{:S(2)}) async-start(), calls=%async_computation.19 | async-start | bytes 3145728 | tf_op jit(solution)/shard_map/reduce_scatter | solution.py:68
  267.3 46.8 %copy-start.6 = (f32[1024,256]{1,0:T(8,128)S(1)}, f32[1024,256]{1,0:T(8,128)}, u32[]{:S(2)}) copy-start(f32[1024,256]{1,0:T(8,128)} %get-tuple-element.588) | copy-start | bytes 3145732
  267.4 81.4 %reduce-scatter.15.cloned.1.call-start = ((), (), s32[]{:S(2)}) async-start(), calls=%async_computation.15 | async-start | bytes 3145728 | tf_op jit(solution)/shard_map/reduce_scatter | solution.py:52
  284.8 64.0 %copy-start.31 = (f32[256]{0:T(256)S(1)}, f32[256]{0:T(256)}, u32[]{:S(2)}) copy-start(f32[256]{0:T(256)} %param.32) | copy-start | bytes 3076
  284.8 89.1 %all-gather.21.cloned.1.call-start = ((), (), s32[]{:S(2)}) async-start(), calls=%async_computation.20 | async-start | bytes 1572864 | tf_op jit(solution)/shard_map/all_gather | solution.py:56
  352.5 34.6 %reduce-scatter.21.cloned.1.call-start = ((), (), s32[]{:S(2)}) async-start(), calls=%async_computation.21 | async-start | bytes 3145728 | tf_op jit(solution)/shard_map/reduce_scatter | solution.py:60
  377.4 67.6 %all-gather.23.cloned.1.call-start = ((), (), s32[]{:S(2)}) async-start(), calls=%async_computation.22 | async-start | bytes 4718592 | tf_op jit(solution)/shard_map/all_gather | solution.py:64
  431.6 51.6 %reduce-scatter.23.cloned.1.call-start = ((), (), s32[]{:S(2)}) async-start(), calls=%async_computation.23 | async-start | bytes 3145728 | tf_op jit(solution)/shard_map/reduce_scatter | solution.py:68
  450.1 439.8 %all-reduce.8.cloned.1.call-start = ((), (), s32[]{:S(2)}) async-start(), calls=%async_computation.24 | async-start | bytes 25165824 | tf_op jit(solution)/shard_map/psum | solution.py:293
  466.7 64.5 %copy-start.9 = (f32[1024,256]{1,0:T(8,128)S(1)}, f32[1024,256]{1,0:T(8,128)}, u32[]{:S(2)}) copy-start(f32[1024,256]{1,0:T(8,128)} %copy-done.8) | copy-start | bytes 3145732
  (35 other events, 278.3 us)
Sparse Core Ops, SparseCore 0:
  20.2 22.1 all-gather.8
  48.7 14.5 reduce-scatter.8
  107.2 10.1 all-gather.10
  121.0 32.9 reduce-scatter.10
  155.4 21.2 all-gather.16
  178.7 21.2 all-gather.12
  202.3 16.8 reduce-scatter.16
  221.5 18.0 reduce-scatter.12
  246.5 14.9 all-gather.18
  263.4 14.8 all-gather.14
  281.1 32.9 reduce-scatter.18
  316.9 31.8 reduce-scatter.14
  352.6 21.2 all-gather.20
  377.5 9.6 reduce-scatter.20
  431.7 13.2 all-gather.22
  450.2 32.9 reduce-scatter.22
  489.0 400.8 all-reduce.7
where the time goes:
time: 917 us; the launch traced here: 907 us
  waiting for transfers between devices  631 us (69%)
  matrix products  98.4 us (11%)
  blocking collectives  68.1 us (7%)
  other arithmetic  51 us (6%)
  local copies, waits for them, and re-layouts  32.4 us (4%)
  between operations  14.8 us (2%)
  loops' own time  10.7 us (1%)
    psum x1, waiting for transfers between devices, shards(): lax.psum((grad_ln1_gain, grad_ln1_shift, grad_w_qkv, grad_b_qv, grad_w_ou...  356 us
    reduce_scatter x2, waiting for transfers between devices, width_reduce(): return lax.psum_scatter(values, 'col', scatter_dimension=1, tiled=True)  58.8 us
    reduce_scatter x2, waiting for transfers between devices, grad_width_reduce(): return lax.psum_scatter(values, 'col', scatter_dimension=1, tiled=True)  40.3 us
    psum x1, blocking collectives, shards(): lax.psum((grad_ln1_gain, grad_ln1_shift, grad_w_qkv, grad_b_qv, grad_w_ou...  39.1 us
    all_gather x2, waiting for transfers between devices, feature_gather(): return lax.all_gather(values, 'col', axis=1, tiled=True)  38 us
    reduce_scatter x2, waiting for transfers between devices, unit_reduce(): return lax.psum_scatter(values, 'row', scatter_dimension=1, tiled=True)  34 us
    all_gather x2, waiting for transfers between devices, grad_feature_gather(): return lax.all_gather(values, 'col', axis=1, tiled=True)  32.5 us
    all_gather x2, waiting for transfers between devices, grad_unit_gather(): return lax.all_gather(values, 'row', axis=1, tiled=True)  27.6 us
  transfers between devices with their start and end apart: 17, of which 17 were waited for; matrix products, arithmetic and copies ran while one was open for 7% of the time, Pallas kernels for 0%

commit v1 on v0

v1 whole, which is shorter than its diff:
```python
import functools

import jax
import jax.numpy as jnp
from jax import lax
from jax.experimental import pallas as pl
from jax.experimental.pallas import tpu as pltpu
from jax.sharding import PartitionSpec as P

HEADS = 16
HEAD_DIM = 64
MAXLEN = 512
BLOCK = 256
PAIR = 6 * HEAD_DIM
EPSILON = 1e-05
FAR = 1e12
BF = jnp.bfloat16
F32 = jnp.float32


def swap_row(values):
    return lax.ppermute(values, "row", [(0, 1), (1, 0)])


def swap_col(values):
    return lax.ppermute(values, "col", [(0, 1), (1, 0)])


def ring_sum(values):
    size = lax.axis_size("dp")
    if size == 1:
        return values
    places = list(range(0, size, 2)) + list(range(size - 1, 0, -2))
    forward = [(places[i], places[(i + 1) % size]) for i in range(size)]
    backward = [(to, start) for start, to in forward]
    place = jnp.array([places.index(i) for i in range(size)], jnp.int32)[lax.axis_index("dp")]
    rows = values.shape[0] // (2 * size)
    result = jnp.zeros(values.shape, values.dtype)
    held = [None, None]
    for step in range(2 * size - 1):
        for way, (perm, sign) in enumerate(((forward, 1), (backward, -1))):
            chunk = (place - sign * step) % size
            offset = (way * size + chunk) * rows
            if step == 0:
                held[way] = lax.dynamic_slice_in_dim(values, offset, rows, 0)
                continue
            held[way] = lax.ppermute(held[way], "dp", perm)
            if step < size:
                held[way] = held[way] + lax.dynamic_slice_in_dim(values, offset, rows, 0)
            if step >= size - 1:
                result = lax.dynamic_update_slice_in_dim(result, held[way], offset, 0)
    return result


def small_sum(values):
    size = lax.axis_size("dp")
    if size & (size - 1):
        return lax.psum(values, "dp")
    bit = 1
    while bit < size:
        values = values + lax.ppermute(values, "dp", [(i, i ^ bit) for i in range(size)])
        bit *= 2
    return values


def nothing(values):
    return values[0, 0].astype(F32) * 0.0


def part(values, index, axis):
    width = values.shape[axis] // 2
    return lax.dynamic_slice_in_dim(values, index * width, width, axis)


def in_order(index, mine, theirs, axis):
    first = jnp.where(index == 0, mine, theirs)
    second = jnp.where(index == 0, theirs, mine)
    return jnp.concatenate([first, second], axis)


def dot(a, b):
    return lax.dot_general(a, b, (((1,), (0,)), ((), ())), preferred_element_type=F32)


def dot_nt(a, b):
    return lax.dot_general(a, b, (((1,), (1,)), ((), ())), preferred_element_type=F32)


def dot_tn(a, b):
    return lax.dot_general(a, b, (((0,), (0,)), ((), ())), preferred_element_type=F32)


def key_start(block):
    return max(0, block * BLOCK - -(-(MAXLEN - 1) // BLOCK) * BLOCK)


def masked_distance(seg_col, seg_row, block):
    low, high = key_start(block), (block + 1) * BLOCK
    rows = slice(block * BLOCK, high)
    query = block * BLOCK + lax.broadcasted_iota(jnp.int32, (BLOCK, high - low), 0)
    key = low + lax.broadcasted_iota(jnp.int32, (BLOCK, high - low), 1)
    allowed = (seg_col[rows, :] == seg_row[:, low:high]) & (key <= query)
    return jnp.where(allowed, (query - key).astype(F32), FAR)


def slope_of(head):
    return jnp.exp2(-8.0 * (jnp.full((1, 1), head, jnp.int32).astype(F32) + 1.0) / HEADS)


def first_head(step, heads):
    return (lax.axis_index("col") * 2 + lax.axis_index("row")) * heads + 2 * step


def forward_kernel(heads, mixed, seg_col, seg_row, context, logsum):
    base = first_head(pl.program_id(0), heads)
    for block in range(mixed.shape[0] // BLOCK):
        low, high = key_start(block), (block + 1) * BLOCK
        rows = slice(block * BLOCK, high)
        distance = masked_distance(seg_col, seg_row, block)
        outs, logs = [], []
        for head in range(2):
            at = head * 3 * HEAD_DIM
            query = mixed[rows, at : at + HEAD_DIM] * BF(HEAD_DIM**-0.5)
            keys = mixed[low:high, at + HEAD_DIM : at + 2 * HEAD_DIM]
            values = mixed[low:high, at + 2 * HEAD_DIM : at + 3 * HEAD_DIM]
            scores = dot_nt(query, keys) - slope_of(base + head) * distance
            ceiling = jnp.max(scores, axis=1, keepdims=True)
            weights = jnp.exp(scores - ceiling)
            total = jnp.sum(weights, axis=1, keepdims=True)
            outs.append(dot(weights.astype(BF), values) / total)
            logs.append(ceiling + jnp.log(total))
        context[rows, :] = jnp.concatenate(outs, 1).astype(BF)
        logsum[0, rows, :] = jnp.concatenate(logs, 1)


def backward_kernel(heads, mixed, seg_col, seg_row, logsum, grad_context, grad_mixed, sums):
    base = first_head(pl.program_id(0), heads)
    sums[...] = jnp.zeros_like(sums)
    for block in range(mixed.shape[0] // BLOCK):
        low, high = key_start(block), (block + 1) * BLOCK
        rows = slice(block * BLOCK, high)
        distance = masked_distance(seg_col, seg_row, block)
        for head in range(2):
            at = head * 3 * HEAD_DIM
            query = mixed[rows, at : at + HEAD_DIM] * BF(HEAD_DIM**-0.5)
            keys = mixed[low:high, at + HEAD_DIM : at + 2 * HEAD_DIM]
            values = mixed[low:high, at + 2 * HEAD_DIM : at + 3 * HEAD_DIM]
            grad = grad_context[rows, head * HEAD_DIM : (head + 1) * HEAD_DIM]
            scores = dot_nt(query, keys) - slope_of(base + head) * distance
            weights = jnp.exp(scores - logsum[0, rows, head : head + 1])
            grad_weights = dot_nt(grad, values)
            inner = jnp.sum(weights * grad_weights, axis=1, keepdims=True)
            grad_scores = (weights * (grad_weights - inner)).astype(BF)
            sums[head, 0, rows, :] = dot(grad_scores, keys) * HEAD_DIM**-0.5
            sums[head, 1, low:high, :] += dot_tn(grad_scores, query)
            sums[head, 2, low:high, :] += dot_tn(weights.astype(BF), grad)
    grad_mixed[...] = jnp.concatenate(
        [sums[head, kind] for head in range(2) for kind in range(3)], 1
    ).astype(BF)


def attention_specs(count):
    return [
        pl.BlockSpec((count, PAIR), lambda i: (0, i)),
        pl.BlockSpec((count, 1), lambda i: (0, 0)),
        pl.BlockSpec((1, count), lambda i: (0, 0)),
    ]


def attend_forward(mixed, seg_col, seg_row):
    count, width = mixed.shape
    pairs = width // PAIR
    return pl.pallas_call(
        functools.partial(forward_kernel, 2 * pairs),
        grid=(pairs,),
        in_specs=attention_specs(count),
        out_specs=[
            pl.BlockSpec((count, 2 * HEAD_DIM), lambda i: (0, i)),
            pl.BlockSpec((1, count, 2), lambda i: (i, 0, 0)),
        ],
        out_shape=[
            jax.ShapeDtypeStruct((count, pairs * 2 * HEAD_DIM), BF),
            jax.ShapeDtypeStruct((pairs, count, 2), F32),
        ],
        compiler_params=pltpu.CompilerParams(vmem_limit_bytes=32 * 2**20),
    )(mixed, seg_col, seg_row)


def attend_backward(mixed, seg_col, seg_row, logsum, grad_context):
    count, width = mixed.shape
    pairs = width // PAIR
    return pl.pallas_call(
        functools.partial(backward_kernel, 2 * pairs),
        grid=(pairs,),
        in_specs=attention_specs(count)
        + [
            pl.BlockSpec((1, count, 2), lambda i: (i, 0, 0)),
            pl.BlockSpec((count, 2 * HEAD_DIM), lambda i: (0, i)),
        ],
        out_specs=pl.BlockSpec((count, PAIR), lambda i: (0, i)),
        out_shape=jax.ShapeDtypeStruct((count, width), BF),
        scratch_shapes=[pltpu.VMEM((2, 3, count, HEAD_DIM), F32)],
        compiler_params=pltpu.CompilerParams(vmem_limit_bytes=32 * 2**20),
    )(mixed, seg_col, seg_row, logsum, grad_context)


def normalize(own, other):
    width = own.shape[1] + other.shape[1]
    center = (jnp.sum(own, axis=1) + jnp.sum(other, axis=1)) / width
    square = (jnp.sum(own * own, axis=1) + jnp.sum(other * other, axis=1)) / width
    scaled = lax.rsqrt(square - center * center + EPSILON)[:, None]
    return ((own - center[:, None]) * scaled, (other - center[:, None]) * scaled, scaled)


def shards(
    tokens,
    lengths,
    ln1_gain,
    ln1_shift,
    w_qkv,
    b_qv,
    w_out,
    b_out,
    ln2_gain,
    ln2_shift,
    w_up,
    b_up,
    w_down,
    b_down,
    cotangent,
):
    row = lax.axis_index("row")
    col = lax.axis_index("col")
    count = tokens.shape[0]
    model = 4 * tokens.shape[1]
    ends = jnp.cumsum(lengths[0])
    places = jnp.arange(count, dtype=jnp.int32)
    segment = jnp.sum((places[:, None] >= ends[None, :]).astype(jnp.int32), axis=1)
    seg_col, seg_row = segment[:, None], segment[None, :]

    def spread(block):
        mine = part(block, row, 0)
        crossed = swap_row(part(block, 1 - row, 0))
        theirs = swap_col(jnp.concatenate([mine, crossed], 1))
        width = mine.shape[1]
        own = in_order(col, mine, theirs[:, :width], 1)
        other = in_order(col, crossed, theirs[:, width:], 1)
        return own, other

    vectors = jnp.stack([ln1_gain, ln1_shift, ln2_gain, ln2_shift, b_out])
    crossed = swap_row(vectors)
    theirs = swap_col(jnp.concatenate([vectors, crossed], 1))
    quarter = vectors.shape[1]
    v_own = in_order(col, vectors, theirs[:, :quarter], 1)
    v_other = in_order(col, crossed, theirs[:, quarter:], 1)

    tok_own, tok_other = spread(tokens)
    w_qkv_o = swap_row(w_qkv)
    w_out_o = swap_row(w_out)
    w_up_o = swap_row(w_up)
    w_down_o = swap_row(w_down)
    cot_own, cot_other = spread(cotangent)

    x_own, x_other = tok_own.astype(F32), tok_other.astype(F32)
    u1_own, u1_other, r1 = normalize(x_own, x_other)
    n1_own = (u1_own * v_own[0] + v_own[1]).astype(BF)
    n1_other = (u1_other * v_other[0] + v_other[1]).astype(BF)
    pair_bias = b_qv.reshape(-1, 2, HEAD_DIM)
    joined_bias = jnp.stack(
        [pair_bias[:, 0], jnp.zeros_like(pair_bias[:, 0]), pair_bias[:, 1]], axis=1
    ).reshape(-1)
    mixed = (dot(n1_own, w_qkv) + dot(n1_other, w_qkv_o) + joined_bias).astype(BF)

    def to_heads(values):
        return in_order(row, part(values, row, 1), swap_row(part(values, 1 - row, 1)), 0)

    def to_tokens(values):
        return in_order(row, part(values, row, 0), swap_row(part(values, 1 - row, 0)), 1)

    head_mixed = to_heads(mixed)
    head_context, logsum = attend_forward(head_mixed, seg_col, seg_row)
    context = to_tokens(head_context)
    out_own = dot(context, w_out)
    got_own = swap_col(out_own.astype(BF))
    out_other = dot(context, w_out_o)
    got_other = swap_col(out_other.astype(BF))
    after_own = x_own + (out_own + got_own.astype(F32)) + v_own[4]
    after_other = x_other + (out_other + got_other.astype(F32)) + v_other[4]
    u2_own, u2_other, r2 = normalize(after_own, after_other)
    n2_own = (u2_own * v_own[2] + v_own[3]).astype(BF)
    n2_other = (u2_other * v_other[2] + v_other[3]).astype(BF)
    preact = dot(n2_own, w_up) + dot(n2_other, w_up_o) + b_up
    active = jax.nn.gelu(preact, approximate=True).astype(BF)

    grad_active = dot_nt(cot_own, w_down) + dot_nt(cot_other, w_down_o)
    unused, gelu_pull = jax.vjp(lambda values: jax.nn.gelu(values, approximate=True), preact)
    grad_pre = gelu_pull(grad_active)[0].astype(BF)
    gn_own = dot_nt(grad_pre, w_up)
    gn_got_own = swap_col(gn_own.astype(BF))
    gn_other = dot_nt(grad_pre, w_up_o)
    gn_got_other = swap_col(gn_other.astype(BF))

    def row_sum(own, other):
        return (own + swap_row(other.astype(BF)).astype(F32)).astype(BF)

    down_own, down_other = dot(active, w_down), dot(active, w_down_o)
    grad_w_down = row_sum(dot_tn(active, cot_own), dot_tn(active, cot_other))
    grad_w_up = row_sum(dot_tn(n2_own, grad_pre), dot_tn(n2_other, grad_pre))
    gain2_own = v_own[2] + nothing(grad_w_down)
    gain2_other = v_other[2] + nothing(grad_w_up)
    grad_w_down, grad_w_up = lax.psum((grad_w_down, grad_w_up), "dp")

    sent = jnp.concatenate([part(down_own, 1 - col, 1), part(down_other, 1 - col, 1)], 1)
    got = swap_col(sent.astype(BF)).astype(F32)
    res_own = part(after_own, col, 1) + part(down_own, col, 1) + got[:, :quarter]
    res_other = part(after_other, col, 1) + part(down_other, col, 1) + got[:, quarter:]
    block_out = (in_order(row, res_own, swap_row(res_other.astype(BF)).astype(F32), 0) + b_down).astype(BF)

    gn_own = gn_own + gn_got_own.astype(F32)
    gn_other = gn_other + gn_got_other.astype(F32)
    e_own, e_other = gn_own * gain2_own, gn_other * gain2_other
    mean_e = (jnp.sum(e_own, axis=1) + jnp.sum(e_other, axis=1))[:, None] / model
    mean_eu = (jnp.sum(e_own * u2_own, axis=1) + jnp.sum(e_other * u2_other, axis=1))[:, None] / model
    ga_own = cot_own.astype(F32) + r2 * (e_own - mean_e - u2_own * mean_eu)
    ga_other = cot_other.astype(F32) + r2 * (e_other - mean_e - u2_other * mean_eu)
    low_own, low_other = ga_own.astype(BF), ga_other.astype(BF)
    grad_context = (dot_nt(low_own, w_out) + dot_nt(low_other, w_out_o)).astype(BF)
    head_grad = attend_backward(head_mixed, seg_col, seg_row, logsum, to_heads(grad_context))
    grad_w_out = row_sum(dot_tn(context, low_own), dot_tn(context, low_other))
    grad_mixed = to_tokens(head_grad)

    g1_own, g1_other = dot_nt(grad_mixed, w_qkv), dot_nt(grad_mixed, w_qkv_o)
    sent = jnp.concatenate([part(g1_own, 1 - col, 1), part(g1_other, 1 - col, 1)], 1)
    got = swap_col(sent.astype(BF)).astype(F32)
    e_own, e_other = g1_own * v_own[0], g1_other * v_other[0]
    sums = jnp.stack(
        [
            jnp.sum(e_own, axis=1) + jnp.sum(e_other, axis=1),
            jnp.sum(e_own * u1_own, axis=1) + jnp.sum(e_other * u1_other, axis=1),
        ]
    )
    sums = (sums + swap_col(sums)) / model
    mean_e, mean_eu = sums[0][:, None], sums[1][:, None]
    g1_own = part(g1_own, col, 1) + got[:, :quarter]
    g1_other = part(g1_other, col, 1) + got[:, quarter:]
    u1_own, u1_other = part(u1_own, col, 1), part(u1_other, col, 1)
    gi_own = part(ga_own, col, 1) + r1 * (
        g1_own * ln1_gain - mean_e - u1_own * mean_eu
    )
    gi_other = part(ga_other, col, 1) + r1 * (
        g1_other * part(v_other[0], col, 0) - mean_e - u1_other * mean_eu
    )
    grad_input = in_order(row, gi_own, swap_row(gi_other), 0)

    def columns(grad, unit):
        return [jnp.sum(part(grad * unit, col, 1), axis=0), jnp.sum(part(grad, col, 1), axis=0)]

    mixed_sums = jnp.sum(grad_mixed, axis=0, dtype=F32).reshape(-1, 3, HEAD_DIM)
    qv_sums = jnp.stack([mixed_sums[:, 0], mixed_sums[:, 2]], axis=1).reshape(-1)
    up_sums = jnp.sum(grad_pre, axis=0, dtype=F32)
    here = columns(gn_own, u2_own) + [jnp.sum(part(ga_own, col, 1), axis=0), qv_sums, up_sums]
    there = columns(gn_other, u2_other) + [jnp.sum(part(ga_other, col, 1), axis=0), qv_sums, up_sums]
    here += [jnp.sum(g1_own * u1_own, axis=0), jnp.sum(g1_own, axis=0)]
    there += [jnp.sum(g1_other * u1_other, axis=0), jnp.sum(g1_other, axis=0)]
    small = jnp.concatenate(here) + swap_row(jnp.concatenate(there))
    small = jnp.concatenate([small, jnp.sum(cotangent, axis=0, dtype=F32)])
    small = small_sum(small.reshape(-1, 128)).reshape(-1)
    grad_w_qkv = row_sum(dot_tn(n1_own, grad_mixed), dot_tn(n1_other, grad_mixed))
    width = grad_w_out.shape[1]
    pieces = [grad_w_qkv[:, at : at + width] for at in range(0, grad_w_qkv.shape[1], width)]
    joined = ring_sum(jnp.concatenate(pieces + [grad_w_out], 0)).astype(F32)
    rows = grad_w_qkv.shape[0]
    grad_w_qkv = jnp.concatenate([joined[at * rows : (at + 1) * rows] for at in range(len(pieces))], 1)
    grad_w_out = joined[len(pieces) * rows :]
    cuts = [0]
    for size in (quarter, quarter, quarter, b_qv.shape[0], b_up.shape[0], quarter, quarter, quarter):
        cuts.append(cuts[-1] + size)
    g_ln2_gain, g_ln2_shift, g_b_out, g_b_qv, g_b_up, g_ln1_gain, g_ln1_shift, g_b_down = [
        small[a:b] for a, b in zip(cuts[:-1], cuts[1:])
    ]
    return (
        block_out,
        grad_input,
        g_ln1_gain,
        g_ln1_shift,
        grad_w_qkv,
        g_b_qv,
        grad_w_out,
        g_b_out,
        g_ln2_gain,
        g_ln2_shift,
        grad_w_up.astype(F32),
        g_b_up,
        grad_w_down.astype(F32),
        g_b_down,
    )


def solution(mesh):
    vector = P(("row", "col"))
    in_specs = (
        P("dp", ("row", "col")),
        P("dp", None),
        vector,
        vector,
        P("row", "col"),
        P("col"),
        P("col", "row"),
        vector,
        vector,
        vector,
        P("row", "col"),
        P("col"),
        P("col", "row"),
        vector,
        P("dp", ("row", "col")),
    )
    out_specs = (
        P("dp", ("row", "col")),
        P("dp", ("row", "col")),
        vector,
        vector,
        P("row", "col"),
        P("col"),
        P("col", "row"),
        vector,
        vector,
        vector,
        P("row", "col"),
        P("col"),
        P("col", "row"),
        vector,
    )
    return jax.shard_map(shards, mesh=mesh, in_specs=in_specs, out_specs=out_specs, check_vma=False)
```

time: 917 us -> 396 us (0.43)
  waiting for transfers between devices: 631 us -> 166 us
  blocking collectives: 68.1 us -> 0 us
  starting transfers between devices: 1.16 us -> 57.7 us
  matrix products: 98.4 us -> 61.9 us
  between operations: 14.8 us -> 37.7 us
  Pallas kernels: 0 us -> 20.2 us
  other arithmetic: 51 us -> 32 us
  local copies, waits for them, and re-layouts: 32.4 us -> 15 us
  loops' own time: 10.7 us -> 0 us
    psum x1, waiting for transfers between devices: 356 us -> 42.2 us  [shards(): grad_w_down, grad_w_up = lax.psum((grad_w_down, grad_w_up), 'dp')]
    reduce_scatter x8 -> x0, waiting for transfers between devices: 154 us -> none  [the longest x2 58.8 us: width_reduce(): return lax.psum_scatter(values, 'col', scatter_dimension=1, tiled=True)]
    ppermute x0 -> x59, waiting for transfers between devices: none -> 124 us  [the longest x28 65 us: ring_sum(): held[way] = lax.ppermute(held[way], 'dp', perm)]
    all_gather x8 -> x0, waiting for transfers between devices: 119 us -> none  [the longest x2 38 us: feature_gather(): return lax.all_gather(values, 'col', axis=1, tiled=True)]
    psum x5 -> x0, blocking collectives: 68.1 us -> none  [the longest x1 39.1 us: shards(): lax.psum((grad_ln1_gain, grad_ln1_shift, grad_w_qkv, grad_b_qv, grad_w_ou...]
    ppermute x0 -> x59, starting transfers between devices: none -> 57.7 us  [the longest x28 40.4 us: ring_sum(): held[way] = lax.ppermute(held[way], 'dp', perm)]
    dot_general x26 -> x24, matrix products: 98.4 us -> 61.9 us  [the longest x8 24.1 us: dot_nt(): lax.dot_general(a, b, (((1,), (1,)), ((), ())), preferred_element_type=F32)]
    pallas_call x0 -> x2, Pallas kernels: none -> 20.2 us  [the longest x1 12.5 us: attend_backward(): pl.pallas_call(functools.partial(backward_kernel, 2 * pairs), grid=(pairs...]
  transfers between devices with their start and end apart: 17 -> 60, of which waited for: 17 -> 31; matrix products, arithmetic and copies ran while one was open for 7% -> 20% of each run, Pallas kernels for 0% -> 5%
where the time goes in v1:
time: 396 us; the launch traced here: 391 us
  waiting for transfers between devices  166 us (42%)
  matrix products  61.9 us (16%)
  starting transfers between devices  57.7 us (15%)
  between operations  37.7 us (10%)
  other arithmetic  32 us (8%)
  Pallas kernels  20.2 us (5%)
  local copies, waits for them, and re-layouts  15 us (4%)
    ppermute x28, waiting for transfers between devices, ring_sum(): held[way] = lax.ppermute(held[way], 'dp', perm)  65 us
    ppermute x10, waiting for transfers between devices, swap_col(): return lax.ppermute(values, 'col', [(0, 1), (1, 0)])  57 us
    psum x1, waiting for transfers between devices, shards(): grad_w_down, grad_w_up = lax.psum((grad_w_down, grad_w_up), 'dp')  42.2 us
    ppermute x28, starting transfers between devices, ring_sum(): held[way] = lax.ppermute(held[way], 'dp', perm)  40.4 us
    dot_general x8, matrix products, dot_nt(): lax.dot_general(a, b, (((1,), (1,)), ((), ())), preferred_element_type=F32)  24.1 us
    dot_general x8, matrix products, dot(): lax.dot_general(a, b, (((1,), (0,)), ((), ())), preferred_element_type=F32)  21.3 us
    dot_general x8, matrix products, dot_tn(): lax.dot_general(a, b, (((0,), (0,)), ((), ())), preferred_element_type=F32)  16.5 us
    pallas_call x1, Pallas kernels, attend_backward(): pl.pallas_call(functools.partial(backward_kernel, 2 * pairs), grid=(pairs...  12.5 us
  transfers between devices with their start and end apart: 60, of which 31 were waited for; matrix products, arithmetic and copies ran while one was open for 20% of the time, Pallas kernels for 5%

profile of v1, /device:TPU:0, one launch (start us, length us, event | category | flops | bytes accessed | tf_op | source)
XLA Modules:
  0.0 390.5 jit_solution(14424082582551194011)
XLA Ops:
  15.3 12.3 %collective-permute-done.1 = bf16[512,512]{1,0:T(8,128)(2,1)S(1)} collective-permute-done((bf16[512,512]{1,0:T(8,128)(2,1)S(1)}, bf16[512,512]{1,0:T(8,128)(2,1)S(1)}, u32[]{:S(2)}, u32[]{:S(2)}) %collective-permute-start.1) | collective-permute-done | bytes 524320 | tf_op jit(solution)/shard_map/ppermute | solution.py:26
  61.4 7.6 %shard_map.263 = (bf16[1024,256]{1,0:T(8,128)(2,1)S(1)}, f32[2,1024,2]{2,1,0:T(8,128)S(1)}) custom-call(bf16[1024,768]{1,0:T(8,128)(2,1)S(1)} %pad_maximum_fusion.2.mixed, s32[1024,1]{1,0:T(8,128)S(1)} %copy.46.seg_col, s32[1,1024]{1,0:T(1,128)S(1)} %bitcast.77), custom_call_target="tpu_custom_call" | custom-call | tf_op jit(solution)/shard_map/pallas_call | solution.py:173
  69.3 4.2 %collective-permute-done.15 = bf16[512,512]{1,0:T(8,128)(2,1)S(1)} collective-permute-done((bf16[512,512]{1,0:T(8,128)(2,1)S(1)}, bf16[512,512]{1,0:T(8,128)(2,1)S(1)}, u32[]{:S(2)}, u32[]{:S(2)}) %collective-permute-start.15) | collective-permute-done | bytes 524320 | tf_op jit(solution)/shard_map/ppermute | solution.py:26
  83.1 8.4 %collective-permute-done.9 = bf16[512,512]{1,0:T(8,128)(2,1)S(1)} collective-permute-done((bf16[512,512]{1,0:T(8,128)(2,1)S(1)}, bf16[512,512]{1,0:T(8,128)(2,1)S(1)}, u32[]{:S(2)}, u32[]{:S(2)}) %collective-permute-start.9) | collective-permute-done | bytes 524320 | tf_op jit(solution)/shard_map/ppermute | solution.py:26
  91.9 9.6 %collective-permute-done.7 = bf16[512,512]{1,0:T(8,128)(2,1)S(1)} collective-permute-done((bf16[512,512]{1,0:T(8,128)(2,1)S(1)}, bf16[512,512]{1,0:T(8,128)(2,1)S(1)}, u32[]{:S(2)}, u32[]{:S(2)}) %collective-permute-start.7) | collective-permute-done | bytes 524320 | tf_op jit(solution)/shard_map/ppermute | solution.py:26
  105.8 3.8 multiply_convert_fusion
  115.4 5.9 %convert_reduce_fusion = (f32[2048]{0:T(1024)S(1)}, bf16[512,2048]{1,0:T(8,128)(2,1)S(1)}) fusion(f32[512,2048]{1,0:T(8,128)S(1)} %get-tuple-element.157, f32[512,2048]{1,0:T(8,128)S(1)} %fusion.27, bf16[2048,512]{1,0:T(8,128)(2,1)} %param.28, bf16[512,256]{1,0:T(8,128)(2,1)S(1)} %get-tuple-element.95, bf16[512,256]{1,0:T(8,128)(2,1)S(1)} %get-tuple-element.94), kind=kOutput, calls=%fused_computation.9 | convolution fusion | flops 1098905600 | bytes 13115392 | tf_op jit(solution)/shard_map/dot_general | solution.py:86
  124.9 4.1 %fusion.56 = (bf16[512,512]{1,0:T(8,128)(2,1)}, f32[512,512]{1,0:T(8,128)}) fusion(bf16[512,2048]{1,0:T(8,128)(2,1)S(1)} %get-tuple-element.164, bf16[512,2048]{1,0:T(8,128)(2,1)} %param.26), kind=kOutput, calls=%fused_computation.242 | convolution fusion | flops 1074003968 | bytes 5767168 | tf_op jit(solution)/shard_map/dot_general | solution.py:86
  130.5 7.0 %collective-permute-done.12 = bf16[512,512]{1,0:T(8,128)(2,1)S(1)} collective-permute-done((bf16[512,512]{1,0:T(8,128)(2,1)S(1)}, bf16[512,512]{1,0:T(8,128)(2,1)S(1)}, u32[]{:S(2)}, u32[]{:S(2)}) %collective-permute-start.12) | collective-permute-done | bytes 524320 | tf_op jit(solution)/shard_map/ppermute | solution.py:26
  137.9 4.1 %fusion.57 = (bf16[512,512]{1,0:T(8,128)(2,1)}, f32[512,512]{1,0:T(8,128)}) fusion(bf16[512,2048]{1,0:T(8,128)(2,1)S(1)} %get-tuple-element.164, bf16[512,2048]{1,0:T(8,128)(2,1)} %collective-permute-done.10), kind=kOutput, calls=%fused_computation.243 | convolution fusion | flops 1074003968 | bytes 5767168 | tf_op jit(solution)/shard_map/dot_general | solution.py:86
  155.5 4.1 %collective-permute-done.18 = bf16[512,512]{1,0:T(8,128)(2,1)} collective-permute-done((bf16[512,512]{1,0:T(8,128)(2,1)}, bf16[512,512]{1,0:T(8,128)(2,1)}, u32[]{:S(2)}, u32[]{:S(2)}) %collective-permute-start.18) | collective-permute-done | bytes 524320 | tf_op jit(solution)/shard_map/ppermute | solution.py:26
  167.6 12.5 %shard_map.264 = bf16[1024,768]{1,0:T(8,128)(2,1)S(1)} custom-call(bf16[1024,768]{1,0:T(8,128)(2,1)S(1)} %pad_maximum_fusion.2.mixed, s32[1024,1]{1,0:T(8,128)S(1)} %copy-done.1, s32[1,1024]{1,0:T(1,128)S(1)} %bitcast.78, f32[2,1024,2]{2,1,0:T(8,128)S(1)} %copy-done.3, bf16[1024,256]{1,0:T(8,128)(2,1)S(1)} %pad_maximum_fusion.13.grad_context), custom_call_target="tpu_custom_call" | custom-call | tf_op jit(solution)/shard_map/pallas_call | solution.py:192
  198.1 10.1 %collective-permute-done.23 = f32[2,512]{1,0:T(2,128)S(1)} collective-permute-done((f32[2,512]{1,0:T(2,128)S(1)}, f32[2,512]{1,0:T(2,128)S(1)}, u32[]{:S(2)}, u32[]{:S(2)}) %collective-permute-start.23) | collective-permute-done | bytes 4128 | tf_op jit(solution)/shard_map/ppermute | solution.py:26
  218.7 6.5 %collective-permute-done.31 = bf16[128,512]{1,0:T(8,128)(2,1)S(1)} collective-permute-done((bf16[128,512]{1,0:T(8,128)(2,1)S(1)}, bf16[128,512]{1,0:T(8,128)(2,1)S(1)}, u32[]{:S(2)}, u32[]{:S(2)}) %collective-permute-start.31) | collective-permute-done | bytes 131104 | tf_op jit(solution)/shard_map/ppermute | solution.py:47
  225.2 6.2 %collective-permute-start.38 = (bf16[128,512]{1,0:T(8,128)(2,1)S(1)}, bf16[128,512]{1,0:T(8,128)(2,1)S(1)}, u32[]{:S(2)}, u32[]{:S(2)}) collective-permute-start(bf16[128,512]{1,0:T(8,128)(2,1)S(1)} %get-tuple-element.85), channel_id=1, source_target_pairs={{8,0},{16,8},{24,16},{28,24},{20,28},{12,20},{4,12},{0,4},{9,1},{1... | collective-permute-start | bytes 393224 | tf_op jit(solution)/shard_map/ppermute | solution.py:47
  232.6 5.0 %collective-permute-done.38 = bf16[128,512]{1,0:T(8,128)(2,1)S(1)} collective-permute-done((bf16[128,512]{1,0:T(8,128)(2,1)S(1)}, bf16[128,512]{1,0:T(8,128)(2,1)S(1)}, u32[]{:S(2)}, u32[]{:S(2)}) %collective-permute-start.38) | collective-permute-done | bytes 131104 | tf_op jit(solution)/shard_map/ppermute | solution.py:47
  237.9 3.9 %collective-permute-start.39 = (bf16[128,512]{1,0:T(8,128)(2,1)S(1)}, bf16[128,512]{1,0:T(8,128)(2,1)S(1)}, u32[]{:S(2)}, u32[]{:S(2)}) collective-permute-start(bf16[128,512]{1,0:T(8,128)(2,1)S(1)} %get-tuple-element.83), channel_id=1, source_target_pairs={{8,0},{16,8},{24,16},{28,24},{20,28},{12,20},{4,12},{0,4},{9,1},{1... | collective-permute-start | bytes 393224 | tf_op jit(solution)/shard_map/ppermute | solution.py:47
  249.4 8.0 %collective-permute-done.40 = bf16[128,512]{1,0:T(8,128)(2,1)S(1)} collective-permute-done((bf16[128,512]{1,0:T(8,128)(2,1)S(1)}, bf16[128,512]{1,0:T(8,128)(2,1)S(1)}, u32[]{:S(2)}, u32[]{:S(2)}) %collective-permute-start.40) | collective-permute-done | bytes 131104 | tf_op jit(solution)/shard_map/ppermute | solution.py:47
  261.0 5.4 %collective-permute-done.41 = bf16[128,512]{1,0:T(8,128)(2,1)S(1)} collective-permute-done((bf16[128,512]{1,0:T(8,128)(2,1)S(1)}, bf16[128,512]{1,0:T(8,128)(2,1)S(1)}, u32[]{:S(2)}, u32[]{:S(2)}) %collective-permute-start.41) | collective-permute-done | bytes 131104 | tf_op jit(solution)/shard_map/ppermute | solution.py:47
  284.5 6.3 %collective-permute-done.44 = bf16[128,512]{1,0:T(8,128)(2,1)S(1)} collective-permute-done((bf16[128,512]{1,0:T(8,128)(2,1)S(1)}, bf16[128,512]{1,0:T(8,128)(2,1)S(1)}, u32[]{:S(2)}, u32[]{:S(2)}) %collective-permute-start.44) | collective-permute-done | bytes 131104 | tf_op jit(solution)/shard_map/ppermute | solution.py:47
  302.0 4.0 %collective-permute-start.50 = (bf16[128,512]{1,0:T(8,128)(2,1)S(1)}, bf16[128,512]{1,0:T(8,128)(2,1)S(1)}, u32[]{:S(2)}, u32[]{:S(2)}) collective-permute-start(bf16[128,512]{1,0:T(8,128)(2,1)S(1)} %collective-permute-done.48), channel_id=1, source_target_pairs={{8,0},{16,8},{24,16},{28,24},{20,28},{12,20},{4,12},{0,4},{9,1},{1... | collective-permute-start | bytes 393224 | tf_op jit(solution)/shard_map/ppermute | solution.py:47
  306.1 4.9 %collective-permute-done.50 = bf16[128,512]{1,0:T(8,128)(2,1)S(1)} collective-permute-done((bf16[128,512]{1,0:T(8,128)(2,1)S(1)}, bf16[128,512]{1,0:T(8,128)(2,1)S(1)}, u32[]{:S(2)}, u32[]{:S(2)}) %collective-permute-start.50) | collective-permute-done | bytes 131104 | tf_op jit(solution)/shard_map/ppermute | solution.py:47
  315.7 42.2 %all-reduce.3.cloned.1.call-done = (bf16[512,2048]{1,0:T(8,128)(2,1)}, bf16[2048,512]{1,0:T(8,128)(2,1)}) async-done(((bf16[512,2048]{1,0:T(8,128)(2,1)}, bf16[2048,512]{1,0:T(8,128)(2,1)}), (bf16[512,2048]{1,0:T(8,128)(2,1)}, bf16[2048,512]{1,0:T(8,128)(2,1)})) %all-reduce.3.cloned.1.call-update) | async-done | bytes 4194320 | tf_op jit(solution)/shard_map/psum | solution.py:311
  357.8 4.3 %convert_element_type.194 = f32[512,2048]{1,0:T(8,128)} convert(bf16[512,2048]{1,0:T(8,128)(2,1)} %get-tuple-element.44) | non-fusion elementwise | flops 1048576 | bytes 6291456 | tf_op jit(solution)/shard_map/convert_element_type | solution.py:392
  (356 shorter events, 162.3 us)
Async XLA Ops:
  9.6 21.1 %collective-permute-start.4 = (bf16[512,1536]{1,0:T(8,128)(2,1)}, bf16[512,1536]{1,0:T(8,128)(2,1)}, u32[]{:S(2)}, u32[]{:S(2)}) collective-permute-start(bf16[512,1536]{1,0:T(8,128)(2,1)} %param.20), channel_id=1, source_target_pairs={{0,2},{2,0},{1,3},{3,1},{4,6},{6,4},{5,7},{7,5},{8,10},{10,8},{9,1... | collective-permute-start | bytes 4718600 | tf_op jit(solution)/shard_map/ppermute | solution.py:22
  13.6 14.1 %collective-permute-start.1 = (bf16[512,512]{1,0:T(8,128)(2,1)S(1)}, bf16[512,512]{1,0:T(8,128)(2,1)S(1)}, u32[]{:S(2)}, u32[]{:S(2)}) collective-permute-start(bf16[512,512]{1,0:T(8,128)(2,1)S(1)} %pad_maximum_fusion.5), channel_id=1, source_target_pairs={{0,1},{1,0},{2,3},{3,2},{4,5},{5,4},{6,7},{7,6},{8,9},{9,8},{10,11... | collective-permute-start | bytes 1572872 | tf_op jit(solution)/shard_map/ppermute | solution.py:26
  34.3 25.5 %collective-permute-start.5 = (bf16[512,768]{1,0:T(8,128)(2,1)}, bf16[512,768]{1,0:T(8,128)(2,1)}, u32[]{:S(2)}, u32[]{:S(2)}) collective-permute-start(bf16[512,768]{1,0:T(8,128)(2,1)} %constant_dynamic-slice_fusion.9), channel_id=1, source_target_pairs={{0,2},{2,0},{1,3},{3,1},{4,6},{6,4},{5,7},{7,5},{8,10},{10,8},{9,1... | collective-permute-start | bytes 2359304 | tf_op jit(solution)/shard_map/ppermute | solution.py:22
  34.3 40.6 %collective-permute-start.8 = (bf16[512,512]{1,0:T(8,128)(2,1)}, bf16[512,512]{1,0:T(8,128)(2,1)}, u32[]{:S(2)}, u32[]{:S(2)}) collective-permute-start(bf16[512,512]{1,0:T(8,128)(2,1)} %param.22), channel_id=1, source_target_pairs={{0,2},{2,0},{1,3},{3,1},{4,6},{6,4},{5,7},{7,5},{8,10},{10,8},{9,1... | collective-permute-start | bytes 1572872 | tf_op jit(solution)/shard_map/ppermute | solution.py:22
  34.8 71.0 %collective-permute-start.10 = (bf16[512,2048]{1,0:T(8,128)(2,1)}, bf16[512,2048]{1,0:T(8,128)(2,1)}, u32[]{:S(2)}, u32[]{:S(2)}) collective-permute-start(bf16[512,2048]{1,0:T(8,128)(2,1)} %param.26), channel_id=1, source_target_pairs={{0,2},{2,0},{1,3},{3,1},{4,6},{6,4},{5,7},{7,5},{8,10},{10,8},{9,1... | collective-permute-start | bytes 6291464 | tf_op jit(solution)/shard_map/ppermute | solution.py:22
  34.8 45.4 %collective-permute-start.11 = (bf16[2048,512]{1,0:T(8,128)(2,1)}, bf16[2048,512]{1,0:T(8,128)(2,1)}, u32[]{:S(2)}, u32[]{:S(2)}) collective-permute-start(bf16[2048,512]{1,0:T(8,128)(2,1)} %param.28), channel_id=1, source_target_pairs={{0,2},{2,0},{1,3},{3,1},{4,6},{6,4},{5,7},{7,5},{8,10},{10,8},{9,1... | collective-permute-start | bytes 6291464 | tf_op jit(solution)/shard_map/ppermute | solution.py:22
  36.0 22.1 %collective-permute-start.14 = (bf16[512,256]{1,0:T(8,128)(2,1)}, bf16[512,256]{1,0:T(8,128)(2,1)}, u32[]{:S(2)}, u32[]{:S(2)}) collective-permute-start(bf16[512,256]{1,0:T(8,128)(2,1)} %get-tuple-element.109), channel_id=1, source_target_pairs={{0,2},{2,0},{1,3},{3,1},{4,6},{6,4},{5,7},{7,5},{8,10},{10,8},{9,1... | collective-permute-start | bytes 786440 | tf_op jit(solution)/shard_map/ppermute | solution.py:22
  59.2 14.4 %collective-permute-start.15 = (bf16[512,512]{1,0:T(8,128)(2,1)S(1)}, bf16[512,512]{1,0:T(8,128)(2,1)S(1)}, u32[]{:S(2)}, u32[]{:S(2)}) collective-permute-start(bf16[512,512]{1,0:T(8,128)(2,1)S(1)} %pad_maximum_fusion.10), channel_id=1, source_target_pairs={{0,1},{1,0},{2,3},{3,2},{4,5},{5,4},{6,7},{7,6},{8,9},{9,8},{10,11... | collective-permute-start | bytes 1572872 | tf_op jit(solution)/shard_map/ppermute | solution.py:26
  76.6 14.9 %collective-permute-start.9 = (bf16[512,512]{1,0:T(8,128)(2,1)S(1)}, bf16[512,512]{1,0:T(8,128)(2,1)S(1)}, u32[]{:S(2)}, u32[]{:S(2)}) collective-permute-start(bf16[512,512]{1,0:T(8,128)(2,1)S(1)} %get-tuple-element.152), channel_id=1, source_target_pairs={{0,1},{1,0},{2,3},{3,2},{4,5},{5,4},{6,7},{7,6},{8,9},{9,8},{10,11... | collective-permute-start | bytes 1572872 | tf_op jit(solution)/shard_map/ppermute | solution.py:26
  78.7 22.8 %collective-permute-start.7 = (bf16[512,512]{1,0:T(8,128)(2,1)S(1)}, bf16[512,512]{1,0:T(8,128)(2,1)S(1)}, u32[]{:S(2)}, u32[]{:S(2)}) collective-permute-start(bf16[512,512]{1,0:T(8,128)(2,1)S(1)} %get-tuple-element.154), channel_id=1, source_target_pairs={{0,1},{1,0},{2,3},{3,2},{4,5},{5,4},{6,7},{7,6},{8,9},{9,8},{10,11... | collective-permute-start | bytes 1572872 | tf_op jit(solution)/shard_map/ppermute | solution.py:26
  122.6 21.9 %collective-permute-start.19 = (bf16[512,2048]{1,0:T(8,128)(2,1)S(1)}, bf16[512,2048]{1,0:T(8,128)(2,1)S(1)}, u32[]{:S(2)}, u32[]{:S(2)}) collective-permute-start(bf16[512,2048]{1,0:T(8,128)(2,1)S(1)} %convolution_convert_fusion.1), channel_id=1, source_target_pairs={{0,2},{2,0},{1,3},{3,1},{4,6},{6,4},{5,7},{7,5},{8,10},{10,8},{9,1... | collective-permute-start | bytes 6291464 | tf_op jit(solution)/shard_map/ppermute | solution.py:22
  122.7 14.8 %collective-permute-start.12 = (bf16[512,512]{1,0:T(8,128)(2,1)S(1)}, bf16[512,512]{1,0:T(8,128)(2,1)S(1)}, u32[]{:S(2)}, u32[]{:S(2)}) collective-permute-start(bf16[512,512]{1,0:T(8,128)(2,1)S(1)} %pad_maximum_fusion.9), channel_id=1, source_target_pairs={{0,1},{1,0},{2,3},{3,2},{4,5},{5,4},{6,7},{7,6},{8,9},{9,8},{10,11... | collective-permute-start | bytes 1572872 | tf_op jit(solution)/shard_map/ppermute | solution.py:26
  124.6 22.5 %collective-permute-start.17 = (bf16[2048,512]{1,0:T(8,128)(2,1)S(1)}, bf16[2048,512]{1,0:T(8,128)(2,1)S(1)}, u32[]{:S(2)}, u32[]{:S(2)}) collective-permute-start(bf16[2048,512]{1,0:T(8,128)(2,1)S(1)} %convolution_convert_fusion.2), channel_id=1, source_target_pairs={{0,2},{2,0},{1,3},{3,1},{4,6},{6,4},{5,7},{7,5},{8,10},{10,8},{9,1... | collective-permute-start | bytes 6291464 | tf_op jit(solution)/shard_map/ppermute | solution.py:22
  129.0 24.8 %collective-permute-start.16 = (bf16[512,512]{1,0:T(8,128)(2,1)}, bf16[512,512]{1,0:T(8,128)(2,1)}, u32[]{:S(2)}, u32[]{:S(2)}) collective-permute-start(bf16[512,512]{1,0:T(8,128)(2,1)} %get-tuple-element.158), channel_id=1, source_target_pairs={{0,1},{1,0},{2,3},{3,2},{4,5},{5,4},{6,7},{7,6},{8,9},{9,8},{10,11... | collective-permute-start | bytes 1572872 | tf_op jit(solution)/shard_map/ppermute | solution.py:26
  142.0 17.7 %collective-permute-start.18 = (bf16[512,512]{1,0:T(8,128)(2,1)}, bf16[512,512]{1,0:T(8,128)(2,1)}, u32[]{:S(2)}, u32[]{:S(2)}) collective-permute-start(bf16[512,512]{1,0:T(8,128)(2,1)} %get-tuple-element.160), channel_id=1, source_target_pairs={{0,1},{1,0},{2,3},{3,2},{4,5},{5,4},{6,7},{7,6},{8,9},{9,8},{10,11... | collective-permute-start | bytes 1572872 | tf_op jit(solution)/shard_map/ppermute | solution.py:26
  152.3 205.6 %all-reduce.3.cloned.1.call-start = ((), (), s32[]{:S(2)}) async-start(), calls=%async_computation | async-start | bytes 8388608 | tf_op jit(solution)/shard_map/psum | solution.py:311
  166.9 17.9 %collective-permute-start.30 = (bf16[512,512]{1,0:T(8,128)(2,1)}, bf16[512,512]{1,0:T(8,128)(2,1)}, u32[]{:S(2)}, u32[]{:S(2)}) collective-permute-start(bf16[512,512]{1,0:T(8,128)(2,1)} %convolution_convert_fusion.3), channel_id=1, source_target_pairs={{0,2},{2,0},{1,3},{3,1},{4,6},{6,4},{5,7},{7,5},{8,10},{10,8},{9,1... | collective-permute-start | bytes 1572872 | tf_op jit(solution)/shard_map/ppermute | solution.py:22
  193.6 14.6 %collective-permute-start.22 = (bf16[512,512]{1,0:T(8,128)(2,1)S(1)}, bf16[512,512]{1,0:T(8,128)(2,1)S(1)}, u32[]{:S(2)}, u32[]{:S(2)}) collective-permute-start(bf16[512,512]{1,0:T(8,128)(2,1)S(1)} %pad_maximum_fusion.14), channel_id=1, source_target_pairs={{0,1},{1,0},{2,3},{3,2},{4,5},{5,4},{6,7},{7,6},{8,9},{9,8},{10,11... | collective-permute-start | bytes 1572872 | tf_op jit(solution)/shard_map/ppermute | solution.py:26
  194.1 14.0 %collective-permute-start.23 = (f32[2,512]{1,0:T(2,128)S(1)}, f32[2,512]{1,0:T(2,128)S(1)}, u32[]{:S(2)}, u32[]{:S(2)}) collective-permute-start(f32[2,512]{1,0:T(2,128)S(1)} %pad_maximum_fusion.22), channel_id=1, source_target_pairs={{0,1},{1,0},{2,3},{3,2},{4,5},{5,4},{6,7},{7,6},{8,9},{9,8},{10,11... | collective-permute-start | bytes 12296 | tf_op jit(solution)/shard_map/ppermute | solution.py:26
  198.1 15.3 %collective-permute-start.29 = (bf16[512,1536]{1,0:T(8,128)(2,1)}, bf16[512,1536]{1,0:T(8,128)(2,1)}, u32[]{:S(2)}, u32[]{:S(2)}) collective-permute-start(bf16[512,1536]{1,0:T(8,128)(2,1)} %convolution_convert_fusion), channel_id=1, source_target_pairs={{0,2},{2,0},{1,3},{3,1},{4,6},{6,4},{5,7},{7,5},{8,10},{10,8},{9,1... | collective-permute-start | bytes 4718600 | tf_op jit(solution)/shard_map/ppermute | solution.py:22
  218.6 23.2 %collective-permute-start.25 = (f32[4352]{0:T(1024)S(1)}, f32[4352]{0:T(1024)S(1)}, u32[]{:S(2)}, u32[]{:S(2)}) collective-permute-start(f32[4352]{0:T(1024)S(1)} %constant_dynamic-update-slice_fusion.17), channel_id=1, source_target_pairs={{0,2},{2,0},{1,3},{3,1},{4,6},{6,4},{5,7},{7,5},{8,10},{10,8},{9,1... | collective-permute-start | bytes 52232 | tf_op jit(solution)/shard_map/ppermute | solution.py:22
  225.2 12.4 %collective-permute-start.38 = (bf16[128,512]{1,0:T(8,128)(2,1)S(1)}, bf16[128,512]{1,0:T(8,128)(2,1)S(1)}, u32[]{:S(2)}, u32[]{:S(2)}) collective-permute-start(bf16[128,512]{1,0:T(8,128)(2,1)S(1)} %get-tuple-element.85), channel_id=1, source_target_pairs={{8,0},{16,8},{24,16},{28,24},{20,28},{12,20},{4,12},{0,4},{9,1},{1... | collective-permute-start | bytes 393224 | tf_op jit(solution)/shard_map/ppermute | solution.py:47
  311.1 53.7 %collective-permute-start.52 = (bf16[128,512]{1,0:T(8,128)(2,1)S(1)}, bf16[128,512]{1,0:T(8,128)(2,1)S(1)}, u32[]{:S(2)}, u32[]{:S(2)}) collective-permute-start(bf16[128,512]{1,0:T(8,128)(2,1)S(1)} %collective-permute-done.50), channel_id=1, source_target_pairs={{8,0},{16,8},{24,16},{28,24},{20,28},{12,20},{4,12},{0,4},{9,1},{1... | collective-permute-start | bytes 393224 | tf_op jit(solution)/shard_map/ppermute | solution.py:47
  315.0 52.0 %collective-permute-start.53 = (bf16[128,512]{1,0:T(8,128)(2,1)S(1)}, bf16[128,512]{1,0:T(8,128)(2,1)S(1)}, u32[]{:S(2)}, u32[]{:S(2)}) collective-permute-start(bf16[128,512]{1,0:T(8,128)(2,1)S(1)} %collective-permute-done.51), channel_id=1, source_target_pairs={{0,8},{8,16},{16,24},{24,28},{28,20},{20,12},{12,4},{4,0},{1,9},{9... | collective-permute-start | bytes 393224 | tf_op jit(solution)/shard_map/ppermute | solution.py:47
  (89 other events, 1205.2 us)
Sparse Core Ops, SparseCore 0:
  182.2 175.6 all-reduce.2

commit v2 on v1

--- a/solution.py
+++ b/solution.py
@@ -308,7 +308,8 @@
     grad_w_up = row_sum(dot_tn(n2_own, grad_pre), dot_tn(n2_other, grad_pre))
     gain2_own = v_own[2] + nothing(grad_w_down)
     gain2_other = v_other[2] + nothing(grad_w_up)
-    grad_w_down, grad_w_up = lax.psum((grad_w_down, grad_w_up), "dp")
+    grad_w_up = lax.psum(grad_w_up, "dp")
+    grad_w_down = ring_sum(grad_w_down)
 
     sent = jnp.concatenate([part(down_own, 1 - col, 1), part(down_other, 1 - col, 1)], 1)
     got = swap_col(sent.astype(BF)).astype(F32)
@@ -368,7 +369,9 @@
     grad_w_qkv = row_sum(dot_tn(n1_own, grad_mixed), dot_tn(n1_other, grad_mixed))
     width = grad_w_out.shape[1]
     pieces = [grad_w_qkv[:, at : at + width] for at in range(0, grad_w_qkv.shape[1], width)]
+    pieces[0] = pieces[0] + nothing(grad_w_down).astype(BF)
     joined = ring_sum(jnp.concatenate(pieces + [grad_w_out], 0)).astype(F32)
+    grad_w_up = grad_w_up.astype(F32) + nothing(joined)
     rows = grad_w_qkv.shape[0]
     grad_w_qkv = jnp.concatenate([joined[at * rows : (at + 1) * rows] for at in range(len(pieces))], 1)
     grad_w_out = joined[len(pieces) * rows :]
@@ -389,7 +392,7 @@
         g_b_out,
         g_ln2_gain,
         g_ln2_shift,
-        grad_w_up.astype(F32),
+        grad_w_up,
         g_b_up,
         grad_w_down.astype(F32),
         g_b_down,

time: 396 us -> 413 us (1.043)
  starting transfers between devices: 57.7 us -> 82.8 us
  waiting for transfers between devices: 166 us -> 150 us
  local copies, waits for them, and re-layouts: 15 us -> 22 us
    psum x1, waiting for transfers between devices: 42.2 us -> 0.01 us  [shards(): grad_w_up = lax.psum(grad_w_up, 'dp')]
    ppermute x28 -> x56, waiting for transfers between devices: 65 us -> 106 us  [ring_sum(): held[way] = lax.ppermute(held[way], 'dp', perm)]
    ppermute x28 -> x56, starting transfers between devices: 40.4 us -> 64.3 us  [ring_sum(): held[way] = lax.ppermute(held[way], 'dp', perm)]
    ppermute x10, waiting for transfers between devices: 57 us -> 43 us  [swap_col(): return lax.ppermute(values, 'col', [(0, 1), (1, 0)])]
    unnamed x116 -> x152, local copies, waits for them, and re-layouts: 2.16 us -> 8.61 us
    select_n x9, other arithmetic: 7.09 us -> 2.7 us  [in_order(): first = jnp.where(index == 0, mine, theirs)]
    add x0 -> x2, other arithmetic: none -> 4.28 us  [the longest x1 4.17 us: shards(): grad_w_up = grad_w_up.astype(F32) + nothing(joined)]
    convert_element_type x1 -> x0, other arithmetic: 4.28 us -> none  [shards(): grad_w_up.astype(F32)]
  transfers between devices with their start and end apart: 60 -> 88, of which waited for: 31 -> 49; matrix products, arithmetic and copies ran while one was open for 20% -> 23% of each run, Pallas kernels for 5% -> 5%
where the time goes in v2:
time: 413 us; the launch traced here: 407 us
  waiting for transfers between devices  150 us (36%)
  starting transfers between devices  82.8 us (20%)
  matrix products  61.9 us (15%)
  between operations  39.9 us (10%)
  other arithmetic  30.3 us (7%)
  local copies, waits for them, and re-layouts  22 us (5%)
  Pallas kernels  20.3 us (5%)
    ppermute x56, waiting for transfers between devices, ring_sum(): held[way] = lax.ppermute(held[way], 'dp', perm)  106 us
    ppermute x56, starting transfers between devices, ring_sum(): held[way] = lax.ppermute(held[way], 'dp', perm)  64.3 us
    ppermute x10, waiting for transfers between devices, swap_col(): return lax.ppermute(values, 'col', [(0, 1), (1, 0)])  43 us
    dot_general x8, matrix products, dot_nt(): lax.dot_general(a, b, (((1,), (1,)), ((), ())), preferred_element_type=F32)  25.8 us
    dot_general x8, matrix products, dot(): lax.dot_general(a, b, (((1,), (0,)), ((), ())), preferred_element_type=F32)  20.7 us
    dot_general x8, matrix products, dot_tn(): lax.dot_general(a, b, (((0,), (0,)), ((), ())), preferred_element_type=F32)  15.4 us
    pallas_call x1, Pallas kernels, attend_backward(): pl.pallas_call(functools.partial(backward_kernel, 2 * pairs), grid=(pairs...  12.4 us
    ppermute x10, starting transfers between devices, swap_col(): return lax.ppermute(values, 'col', [(0, 1), (1, 0)])  10.5 us
  transfers between devices with their start and end apart: 88, of which 49 were waited for; matrix products, arithmetic and copies ran while one was open for 23% of the time, Pallas kernels for 5%

profile of v2, /device:TPU:0, one launch (start us, length us, event | category | flops | bytes accessed | tf_op | source)
XLA Modules:
  0.0 406.9 jit_solution(6507948869770738197)
XLA Ops:
  15.4 12.3 %collective-permute-done.1 = bf16[512,512]{1,0:T(8,128)(2,1)S(1)} collective-permute-done((bf16[512,512]{1,0:T(8,128)(2,1)S(1)}, bf16[512,512]{1,0:T(8,128)(2,1)S(1)}, u32[]{:S(2)}, u32[]{:S(2)}) %collective-permute-start.1) | collective-permute-done | bytes 524320 | tf_op jit(solution)/shard_map/ppermute | solution.py:26
  59.5 7.9 %shard_map.272 = (bf16[1024,256]{1,0:T(8,128)(2,1)S(1)}, f32[2,1024,2]{2,1,0:T(8,128)S(1)}) custom-call(bf16[1024,768]{1,0:T(8,128)(2,1)S(1)} %pad_maximum_fusion.2.mixed, s32[1024,1]{1,0:T(8,128)S(1)} %copy.47.seg_col, s32[1,1024]{1,0:T(1,128)S(1)} %bitcast.79), custom_call_target="tpu_custom_call" | custom-call | tf_op jit(solution)/shard_map/pallas_call | solution.py:173
  67.7 3.9 collective-permute-done.15
  80.3 8.3 %collective-permute-done.9 = bf16[512,512]{1,0:T(8,128)(2,1)S(1)} collective-permute-done((bf16[512,512]{1,0:T(8,128)(2,1)S(1)}, bf16[512,512]{1,0:T(8,128)(2,1)S(1)}, u32[]{:S(2)}, u32[]{:S(2)}) %collective-permute-start.9) | collective-permute-done | bytes 524320 | tf_op jit(solution)/shard_map/ppermute | solution.py:26
  89.0 9.5 %collective-permute-done.7 = bf16[512,512]{1,0:T(8,128)(2,1)S(1)} collective-permute-done((bf16[512,512]{1,0:T(8,128)(2,1)S(1)}, bf16[512,512]{1,0:T(8,128)(2,1)S(1)}, u32[]{:S(2)}, u32[]{:S(2)}) %collective-permute-start.7) | collective-permute-done | bytes 524320 | tf_op jit(solution)/shard_map/ppermute | solution.py:26
  102.9 3.8 multiply_convert_fusion
  113.9 6.2 %convert_reduce_fusion = (f32[2048]{0:T(1024)}, bf16[512,2048]{1,0:T(8,128)(2,1)S(1)}) fusion(f32[512,2048]{1,0:T(8,128)S(1)} %get-tuple-element.172, f32[512,2048]{1,0:T(8,128)S(1)} %fusion.27, bf16[2048,512]{1,0:T(8,128)(2,1)} %param.29, bf16[512,256]{1,0:T(8,128)(2,1)S(1)} %get-tuple-element.110, bf16[512,256]{1,0:T(8,128)(2,1)S(1)} %get-tuple-element.109), kind=kOutput, calls=%fused_computation.10 | convolution fusion | flops 1098905600 | bytes 13115392 | tf_op jit(solution)/shard_map/dot_general | solution.py:86
  124.6 4.1 fusion.55
  130.5 4.1 %fusion.56 = (bf16[512,512]{1,0:T(8,128)(2,1)}, f32[512,512]{1,0:T(8,128)}) fusion(bf16[512,2048]{1,0:T(8,128)(2,1)S(1)} %get-tuple-element.179, bf16[512,2048]{1,0:T(8,128)(2,1)} %collective-permute-done.10), kind=kOutput, calls=%fused_computation.276 | convolution fusion | flops 1074003968 | bytes 5767168 | tf_op jit(solution)/shard_map/dot_general | solution.py:86
  139.0 3.7 add_convert_fusion.1
  150.0 4.1 collective-permute-done.18
  161.1 6.2 %collective-permute-done.30 = bf16[128,512]{1,0:T(8,128)(2,1)S(1)} collective-permute-done((bf16[128,512]{1,0:T(8,128)(2,1)S(1)}, bf16[128,512]{1,0:T(8,128)(2,1)S(1)}, u32[]{:S(2)}, u32[]{:S(2)}) %collective-permute-start.30) | collective-permute-done | bytes 131104 | tf_op jit(solution)/shard_map/ppermute | solution.py:47
  167.3 5.0 %collective-permute-start.37 = (bf16[128,512]{1,0:T(8,128)(2,1)S(1)}, bf16[128,512]{1,0:T(8,128)(2,1)S(1)}, u32[]{:S(2)}, u32[]{:S(2)}) collective-permute-start(bf16[128,512]{1,0:T(8,128)(2,1)S(1)} %get-tuple-element.100), channel_id=1, source_target_pairs={{8,0},{16,8},{24,16},{28,24},{20,28},{12,20},{4,12},{0,4},{9,1},{1... | collective-permute-start | bytes 393224 | tf_op jit(solution)/shard_map/ppermute | solution.py:47
  173.8 6.9 %collective-permute-done.37 = bf16[128,512]{1,0:T(8,128)(2,1)S(1)} collective-permute-done((bf16[128,512]{1,0:T(8,128)(2,1)S(1)}, bf16[128,512]{1,0:T(8,128)(2,1)S(1)}, u32[]{:S(2)}, u32[]{:S(2)}) %collective-permute-start.37) | collective-permute-done | bytes 131104 | tf_op jit(solution)/shard_map/ppermute | solution.py:47
  180.9 4.9 %collective-permute-start.38 = (bf16[128,512]{1,0:T(8,128)(2,1)S(1)}, bf16[128,512]{1,0:T(8,128)(2,1)S(1)}, u32[]{:S(2)}, u32[]{:S(2)}) collective-permute-start(bf16[128,512]{1,0:T(8,128)(2,1)S(1)} %get-tuple-element.98), channel_id=1, source_target_pairs={{8,0},{16,8},{24,16},{28,24},{20,28},{12,20},{4,12},{0,4},{9,1},{1... | collective-permute-start | bytes 393224 | tf_op jit(solution)/shard_map/ppermute | solution.py:47
  199.6 12.4 %shard_map.273 = bf16[1024,768]{1,0:T(8,128)(2,1)S(1)} custom-call(bf16[1024,768]{1,0:T(8,128)(2,1)S(1)} %pad_maximum_fusion.2.mixed, s32[1024,1]{1,0:T(8,128)S(1)} %copy.47.seg_col, s32[1,1024]{1,0:T(1,128)S(1)} %bitcast.80, f32[2,1024,2]{2,1,0:T(8,128)S(1)} %get-tuple-element.17.logsum, bf16[1024,256]{1,0:T(8,128)(2,1)S(1)} %pad_maximum_fusion.13.grad_context), custom_call_target="tpu_custom_call" | custom-call | tf_op jit(solution)/shard_map/pallas_call | solution.py:192
  233.1 3.8 multiply_reduce_fusion.6
  250.3 5.2 %collective-permute-done.45 = bf16[128,512]{1,0:T(8,128)(2,1)S(1)} collective-permute-done((bf16[128,512]{1,0:T(8,128)(2,1)S(1)}, bf16[128,512]{1,0:T(8,128)(2,1)S(1)}, u32[]{:S(2)}, u32[]{:S(2)}) %collective-permute-start.45) | collective-permute-done | bytes 131104 | tf_op jit(solution)/shard_map/ppermute | solution.py:47
  257.6 9.3 %collective-permute-done.47 = bf16[128,512]{1,0:T(8,128)(2,1)S(1)} collective-permute-done((bf16[128,512]{1,0:T(8,128)(2,1)S(1)}, bf16[128,512]{1,0:T(8,128)(2,1)S(1)}, u32[]{:S(2)}, u32[]{:S(2)}) %collective-permute-start.47) | collective-permute-done | bytes 131104 | tf_op jit(solution)/shard_map/ppermute | solution.py:47
  280.2 4.0 collective-permute-done.53
  289.8 4.6 %collective-permute-done.57 = bf16[128,512]{1,0:T(8,128)(2,1)S(1)} collective-permute-done((bf16[128,512]{1,0:T(8,128)(2,1)S(1)}, bf16[128,512]{1,0:T(8,128)(2,1)S(1)}, u32[]{:S(2)}, u32[]{:S(2)}) %collective-permute-start.57) | collective-permute-done | bytes 131104 | tf_op jit(solution)/shard_map/ppermute | solution.py:47
  308.6 4.0 collective-permute-done.66
  387.2 3.7 collective-permute-done.86
  395.5 4.2 %convert_add_fusion = f32[512,2048]{1,0:T(8,128)} fusion(bf16[512,2048]{1,0:T(8,128)(2,1)} %all-reduce.2.cloned.1.call-done, f32[]{:T(128)} %bitcast.37), kind=kLoop, calls=%fused_computation.9 | loop fusion | flops 2097152 | bytes 6291460 | tf_op jit(solution)/shard_map/add | solution.py:374
  (474 shorter events, 225.1 us)
Async XLA Ops:
  9.6 19.7 %collective-permute-start.4 = (bf16[512,1536]{1,0:T(8,128)(2,1)}, bf16[512,1536]{1,0:T(8,128)(2,1)}, u32[]{:S(2)}, u32[]{:S(2)}) collective-permute-start(bf16[512,1536]{1,0:T(8,128)(2,1)} %param.21), channel_id=1, source_target_pairs={{0,2},{2,0},{1,3},{3,1},{4,6},{6,4},{5,7},{7,5},{8,10},{10,8},{9,1... | collective-permute-start | bytes 4718600 | tf_op jit(solution)/shard_map/ppermute | solution.py:22
  13.6 14.1 %collective-permute-start.1 = (bf16[512,512]{1,0:T(8,128)(2,1)S(1)}, bf16[512,512]{1,0:T(8,128)(2,1)S(1)}, u32[]{:S(2)}, u32[]{:S(2)}) collective-permute-start(bf16[512,512]{1,0:T(8,128)(2,1)S(1)} %pad_maximum_fusion.5), channel_id=1, source_target_pairs={{0,1},{1,0},{2,3},{3,2},{4,5},{5,4},{6,7},{7,6},{8,9},{9,8},{10,11... | collective-permute-start | bytes 1572872 | tf_op jit(solution)/shard_map/ppermute | solution.py:26
  32.9 25.0 %collective-permute-start.5 = (bf16[512,768]{1,0:T(8,128)(2,1)}, bf16[512,768]{1,0:T(8,128)(2,1)}, u32[]{:S(2)}, u32[]{:S(2)}) collective-permute-start(bf16[512,768]{1,0:T(8,128)(2,1)} %constant_dynamic-slice_fusion.11), channel_id=1, source_target_pairs={{0,2},{2,0},{1,3},{3,1},{4,6},{6,4},{5,7},{7,5},{8,10},{10,8},{9,1... | collective-permute-start | bytes 2359304 | tf_op jit(solution)/shard_map/ppermute | solution.py:22
  32.9 39.0 %collective-permute-start.8 = (bf16[512,512]{1,0:T(8,128)(2,1)}, bf16[512,512]{1,0:T(8,128)(2,1)}, u32[]{:S(2)}, u32[]{:S(2)}) collective-permute-start(bf16[512,512]{1,0:T(8,128)(2,1)} %param.23), channel_id=1, source_target_pairs={{0,2},{2,0},{1,3},{3,1},{4,6},{6,4},{5,7},{7,5},{8,10},{10,8},{9,1... | collective-permute-start | bytes 1572872 | tf_op jit(solution)/shard_map/ppermute | solution.py:22
  33.4 69.4 %collective-permute-start.10 = (bf16[512,2048]{1,0:T(8,128)(2,1)}, bf16[512,2048]{1,0:T(8,128)(2,1)}, u32[]{:S(2)}, u32[]{:S(2)}) collective-permute-start(bf16[512,2048]{1,0:T(8,128)(2,1)} %param.27), channel_id=1, source_target_pairs={{0,2},{2,0},{1,3},{3,1},{4,6},{6,4},{5,7},{7,5},{8,10},{10,8},{9,1... | collective-permute-start | bytes 6291464 | tf_op jit(solution)/shard_map/ppermute | solution.py:22
  33.4 43.9 %collective-permute-start.11 = (bf16[2048,512]{1,0:T(8,128)(2,1)}, bf16[2048,512]{1,0:T(8,128)(2,1)}, u32[]{:S(2)}, u32[]{:S(2)}) collective-permute-start(bf16[2048,512]{1,0:T(8,128)(2,1)} %param.29), channel_id=1, source_target_pairs={{0,2},{2,0},{1,3},{3,1},{4,6},{6,4},{5,7},{7,5},{8,10},{10,8},{9,1... | collective-permute-start | bytes 6291464 | tf_op jit(solution)/shard_map/ppermute | solution.py:22
  34.0 23.3 %collective-permute-start.14 = (bf16[512,256]{1,0:T(8,128)(2,1)S(1)}, bf16[512,256]{1,0:T(8,128)(2,1)S(1)}, u32[]{:S(2)}, u32[]{:S(2)}) collective-permute-start(bf16[512,256]{1,0:T(8,128)(2,1)S(1)} %get-tuple-element.124), channel_id=1, source_target_pairs={{0,2},{2,0},{1,3},{3,1},{4,6},{6,4},{5,7},{7,5},{8,10},{10,8},{9,1... | collective-permute-start | bytes 786440 | tf_op jit(solution)/shard_map/ppermute | solution.py:22
  57.3 14.3 %collective-permute-start.15 = (bf16[512,512]{1,0:T(8,128)(2,1)S(1)}, bf16[512,512]{1,0:T(8,128)(2,1)S(1)}, u32[]{:S(2)}, u32[]{:S(2)}) collective-permute-start(bf16[512,512]{1,0:T(8,128)(2,1)S(1)} %pad_maximum_fusion.10), channel_id=1, source_target_pairs={{0,1},{1,0},{2,3},{3,2},{4,5},{5,4},{6,7},{7,6},{8,9},{9,8},{10,11... | collective-permute-start | bytes 1572872 | tf_op jit(solution)/shard_map/ppermute | solution.py:26
  73.7 14.9 %collective-permute-start.9 = (bf16[512,512]{1,0:T(8,128)(2,1)S(1)}, bf16[512,512]{1,0:T(8,128)(2,1)S(1)}, u32[]{:S(2)}, u32[]{:S(2)}) collective-permute-start(bf16[512,512]{1,0:T(8,128)(2,1)S(1)} %get-tuple-element.167), channel_id=1, source_target_pairs={{0,1},{1,0},{2,3},{3,2},{4,5},{5,4},{6,7},{7,6},{8,9},{9,8},{10,11... | collective-permute-start | bytes 1572872 | tf_op jit(solution)/shard_map/ppermute | solution.py:26
  75.8 22.7 %collective-permute-start.7 = (bf16[512,512]{1,0:T(8,128)(2,1)S(1)}, bf16[512,512]{1,0:T(8,128)(2,1)S(1)}, u32[]{:S(2)}, u32[]{:S(2)}) collective-permute-start(bf16[512,512]{1,0:T(8,128)(2,1)S(1)} %get-tuple-element.169), channel_id=1, source_target_pairs={{0,1},{1,0},{2,3},{3,2},{4,5},{5,4},{6,7},{7,6},{8,9},{9,8},{10,11... | collective-permute-start | bytes 1572872 | tf_op jit(solution)/shard_map/ppermute | solution.py:26
  113.2 16.9 %collective-permute-start.12 = (bf16[512,512]{1,0:T(8,128)(2,1)S(1)}, bf16[512,512]{1,0:T(8,128)(2,1)S(1)}, u32[]{:S(2)}, u32[]{:S(2)}) collective-permute-start(bf16[512,512]{1,0:T(8,128)(2,1)S(1)} %pad_maximum_fusion.9), channel_id=1, source_target_pairs={{0,1},{1,0},{2,3},{3,2},{4,5},{5,4},{6,7},{7,6},{8,9},{9,8},{10,11... | collective-permute-start | bytes 1572872 | tf_op jit(solution)/shard_map/ppermute | solution.py:26
  121.4 15.0 %collective-permute-start.19 = (bf16[512,2048]{1,0:T(8,128)(2,1)S(1)}, bf16[512,2048]{1,0:T(8,128)(2,1)S(1)}, u32[]{:S(2)}, u32[]{:S(2)}) collective-permute-start(bf16[512,2048]{1,0:T(8,128)(2,1)S(1)} %convolution_convert_fusion.1), channel_id=1, source_target_pairs={{0,2},{2,0},{1,3},{3,1},{4,6},{6,4},{5,7},{7,5},{8,10},{10,8},{9,1... | collective-permute-start | bytes 6291464 | tf_op jit(solution)/shard_map/ppermute | solution.py:22
  124.1 14.9 %collective-permute-start.17 = (bf16[2048,512]{1,0:T(8,128)(2,1)}, bf16[2048,512]{1,0:T(8,128)(2,1)}, u32[]{:S(2)}, u32[]{:S(2)}) collective-permute-start(bf16[2048,512]{1,0:T(8,128)(2,1)} %convolution_convert_fusion.2), channel_id=1, source_target_pairs={{0,2},{2,0},{1,3},{3,1},{4,6},{6,4},{5,7},{7,5},{8,10},{10,8},{9,1... | collective-permute-start | bytes 6291464 | tf_op jit(solution)/shard_map/ppermute | solution.py:22
  128.7 19.3 %collective-permute-start.16 = (bf16[512,512]{1,0:T(8,128)(2,1)}, bf16[512,512]{1,0:T(8,128)(2,1)}, u32[]{:S(2)}, u32[]{:S(2)}) collective-permute-start(bf16[512,512]{1,0:T(8,128)(2,1)} %get-tuple-element.173), channel_id=1, source_target_pairs={{0,1},{1,0},{2,3},{3,2},{4,5},{5,4},{6,7},{7,6},{8,9},{9,8},{10,11... | collective-permute-start | bytes 1572872 | tf_op jit(solution)/shard_map/ppermute | solution.py:26
  134.6 19.5 %collective-permute-start.18 = (bf16[512,512]{1,0:T(8,128)(2,1)}, bf16[512,512]{1,0:T(8,128)(2,1)}, u32[]{:S(2)}, u32[]{:S(2)}) collective-permute-start(bf16[512,512]{1,0:T(8,128)(2,1)} %get-tuple-element.175), channel_id=1, source_target_pairs={{0,1},{1,0},{2,3},{3,2},{4,5},{5,4},{6,7},{7,6},{8,9},{9,8},{10,11... | collective-permute-start | bytes 1572872 | tf_op jit(solution)/shard_map/ppermute | solution.py:26
  145.7 249.7 %all-reduce.2.cloned.1.call-start = ((), (), s32[]{:S(2)}) async-start(), calls=%async_computation | async-start | bytes 4194304 | tf_op jit(solution)/shard_map/psum | solution.py:311
  185.9 34.9 %collective-permute-start.58 = (bf16[512,512]{1,0:T(8,128)(2,1)S(1)}, bf16[512,512]{1,0:T(8,128)(2,1)S(1)}, u32[]{:S(2)}, u32[]{:S(2)}) collective-permute-start(bf16[512,512]{1,0:T(8,128)(2,1)S(1)} %convolution_convert_fusion.3), channel_id=1, source_target_pairs={{0,2},{2,0},{1,3},{3,1},{4,6},{6,4},{5,7},{7,5},{8,10},{10,8},{9,1... | collective-permute-start | bytes 1572872 | tf_op jit(solution)/shard_map/ppermute | solution.py:22
  197.2 14.8 %collective-permute-start.40 = (bf16[128,512]{1,0:T(8,128)(2,1)S(1)}, bf16[128,512]{1,0:T(8,128)(2,1)S(1)}, u32[]{:S(2)}, u32[]{:S(2)}) collective-permute-start(bf16[128,512]{1,0:T(8,128)(2,1)S(1)} %get-tuple-element.94), channel_id=1, source_target_pairs={{8,0},{16,8},{24,16},{28,24},{20,28},{12,20},{4,12},{0,4},{9,1},{1... | collective-permute-start | bytes 393224 | tf_op jit(solution)/shard_map/ppermute | solution.py:47
  214.2 14.1 %collective-permute-start.21 = (bf16[512,768]{1,0:T(8,128)(2,1)S(1)}, bf16[512,768]{1,0:T(8,128)(2,1)S(1)}, u32[]{:S(2)}, u32[]{:S(2)}) collective-permute-start(bf16[512,768]{1,0:T(8,128)(2,1)S(1)} %constant_dynamic-slice_fusion.6), channel_id=1, source_target_pairs={{0,2},{2,0},{1,3},{3,1},{4,6},{6,4},{5,7},{7,5},{8,10},{10,8},{9,1... | collective-permute-start | bytes 2359304 | tf_op jit(solution)/shard_map/ppermute | solution.py:22
  226.3 15.6 %collective-permute-start.43 = (bf16[128,512]{1,0:T(8,128)(2,1)}, bf16[128,512]{1,0:T(8,128)(2,1)S(1)}, u32[]{:S(2)}, u32[]{:S(2)}) collective-permute-start(bf16[128,512]{1,0:T(8,128)(2,1)} %get-tuple-element.89), channel_id=1, source_target_pairs={{8,0},{16,8},{24,16},{28,24},{20,28},{12,20},{4,12},{0,4},{9,1},{1... | collective-permute-start | bytes 393224 | tf_op jit(solution)/shard_map/ppermute | solution.py:47
  228.0 16.6 %collective-permute-start.44 = (bf16[128,512]{1,0:T(8,128)(2,1)}, bf16[128,512]{1,0:T(8,128)(2,1)}, u32[]{:S(2)}, u32[]{:S(2)}) collective-permute-start(bf16[128,512]{1,0:T(8,128)(2,1)} %get-tuple-element.51), channel_id=1, source_target_pairs={{0,8},{8,16},{16,24},{24,28},{28,20},{20,12},{12,4},{4,0},{1,9},{9... | collective-permute-start | bytes 393224 | tf_op jit(solution)/shard_map/ppermute | solution.py:47
  238.1 37.0 %collective-permute-start.22 = (bf16[512,512]{1,0:T(8,128)(2,1)}, bf16[512,512]{1,0:T(8,128)(2,1)}, u32[]{:S(2)}, u32[]{:S(2)}) collective-permute-start(bf16[512,512]{1,0:T(8,128)(2,1)} %pad_maximum_fusion.14), channel_id=1, source_target_pairs={{0,1},{1,0},{2,3},{3,2},{4,5},{5,4},{6,7},{7,6},{8,9},{9,8},{10,11... | collective-permute-start | bytes 1572872 | tf_op jit(solution)/shard_map/ppermute | solution.py:26
  241.8 57.0 %collective-permute-start.29 = (bf16[512,1536]{1,0:T(8,128)(2,1)}, bf16[512,1536]{1,0:T(8,128)(2,1)S(1)}, u32[]{:S(2)}, u32[]{:S(2)}) collective-permute-start(bf16[512,1536]{1,0:T(8,128)(2,1)} %convolution_convert_fusion), channel_id=1, source_target_pairs={{0,2},{2,0},{1,3},{3,1},{4,6},{6,4},{5,7},{7,5},{8,10},{10,8},{9,1... | collective-permute-start | bytes 4718600 | tf_op jit(solution)/shard_map/ppermute | solution.py:22
  278.0 20.5 %collective-permute-start.24 = (f32[512,256]{1,0:T(8,128)S(1)}, f32[512,256]{1,0:T(8,128)S(1)}, u32[]{:S(2)}, u32[]{:S(2)}) collective-permute-start(f32[512,256]{1,0:T(8,128)S(1)} %get-tuple-element.67), channel_id=1, source_target_pairs={{0,2},{2,0},{1,3},{3,1},{4,6},{6,4},{5,7},{7,5},{8,10},{10,8},{9,1... | collective-permute-start | bytes 1572872 | tf_op jit(solution)/shard_map/ppermute | solution.py:22
  (135 other events, 1822.0 us)
Sparse Core Ops, SparseCore 0:
  150.8 119.5 all-reduce.1
